TPU v7x, 128 devices: a whole 4x4x4 slice. The times are simulated.
128 devices in a mesh: row: 8 (over x_hi, y), col: 16 (over x_lo, z, core).
Axes of the slice: x: 4 (x_hi: 2, x_lo: 2; x = x_hi * 2 + x_lo), y: 4, z: 4, core: 2. Of those that a mesh axis runs over, the one named last changes fastest.
Arguments:
- features: bfloat16 [131072, 128], P(('col', 'row')), may hold values from -6 to 6
- weight: bfloat16 [128, 256], replicated, may hold values from -0.5 to 0.5
- bias: float32 [256], replicated, may hold values from -4 to 4
- adjacency: bfloat16 [8, 16, 256, 128, 128], P('row', 'col'), may hold values from -0.09375 to 0.09375
- block_rows: int32 [8, 16, 256], P('row', 'col'), may hold values from 0 to 127, as said below
- block_cols: int32 [8, 16, 256], P('row', 'col'), may hold values from 0 to 63, as said below
- block_count: int32 [8, 16], P('row', 'col'), may hold values from 128 to 256, as said below
- cotangent: bfloat16 [131072, 256], P(('row', 'col')), may hold values from -6 to 6
- relu_mask: int32 [131072, 256], P(('row', 'col')), may hold values 0 or 1
Outputs:
- output: bfloat16 [131072, 256], P(('row', 'col'))
- grad_features: bfloat16 [131072, 128], P(('col', 'row'))
- grad_weight: float32 [128, 256], replicated
- grad_bias: float32 [256], replicated
Inputs may be any that keep to these rules, and one draw needn't show every extreme that they name: Each device's block_rows lie in 0 to 1024 * 16 / 128 - 1; the (row, col) pairs of one device's slots are distinct. Each device's block_cols lie in 0 to 1024 * 8 / 128 - 1; see block_rows. `block_count`: slots at or past a device's count hold values that are not part of A; some device has all 256 slots live.
All inputs are finite; a program needn't handle non-finite values. No bound on the sum of `relu_mask` on one device may be relied on, other than what follows from the above.
Results may differ from a plain program's by a relative error of at most 0.0049.
Values may be sent and summed in bfloat16 or wider, within the bound.
A program may use at most 192 MiB of HBM per device.

v0:
```python
import jax
import jax.numpy as jnp
from jax import lax
from jax.sharding import PartitionSpec as P


def local(
    features, weight, bias, adjacency, block_rows, block_cols, block_count, cotangent, relu_mask
):
    blocks = adjacency[0, 0]
    rows_index = block_rows[0, 0]
    cols_index = block_cols[0, 0]
    slots = blocks.shape[0]
    width = blocks.shape[1]
    feat_width = features.shape[1]
    alive_slots = (jnp.arange(slots, dtype=jnp.int32) < block_count[0, 0]).astype(jnp.float32)
    own_rows = relu_mask.shape[0]
    row_segments = own_rows * lax.axis_size("col") // width
    column_feats = lax.all_gather(features, "row", axis=0, tiled=True)
    col_segments = column_feats.shape[0] // width
    feat_blocks = column_feats.reshape(col_segments, width, feat_width)
    picked = jnp.take(feat_blocks, cols_index, axis=0)
    products = jnp.einsum("kab,kbf->kaf", blocks, picked, preferred_element_type=jnp.float32)
    products = products * alive_slots[:, None, None]
    row_part = jax.ops.segment_sum(products, rows_index, num_segments=row_segments).reshape(
        -1, feat_width
    )
    summed_rows = lax.psum_scatter(row_part, "col", scatter_dimension=0, tiled=True)
    aggregated = summed_rows.astype(jnp.bfloat16)
    mask_float = relu_mask.astype(jnp.float32)
    preact = jnp.dot(aggregated, weight, preferred_element_type=jnp.float32) + bias
    output = (preact * mask_float).astype(jnp.bfloat16)
    grad_pre = (cotangent.astype(jnp.float32) * mask_float).astype(jnp.bfloat16)
    local_weight = jnp.dot(aggregated.T, grad_pre, preferred_element_type=jnp.float32)
    local_bias = jnp.sum(grad_pre.astype(jnp.float32), axis=0)
    grad_weight, grad_bias = lax.psum((local_weight, local_bias), ("row", "col"))
    grad_rows = lax.all_gather(grad_pre, "col", axis=0, tiled=True)
    grad_proj = jnp.dot(grad_rows, weight.T, preferred_element_type=jnp.float32).astype(
        jnp.bfloat16
    )
    proj_blocks = grad_proj.reshape(row_segments, width, feat_width)
    picked_back = jnp.take(proj_blocks, rows_index, axis=0)
    backward = jnp.einsum("kab,kaf->kbf", blocks, picked_back, preferred_element_type=jnp.float32)
    backward = backward * alive_slots[:, None, None]
    col_part = jax.ops.segment_sum(backward, cols_index, num_segments=col_segments).reshape(
        -1, feat_width
    )
    summed_cols = lax.psum_scatter(col_part, "row", scatter_dimension=0, tiled=True)
    grad_features = summed_cols.astype(jnp.bfloat16)
    return (output, grad_features, grad_weight, grad_bias)


def solution(mesh):
    in_specs = (
        P(("col", "row"), None),
        P(),
        P(),
        P("row", "col", None, None, None),
        P("row", "col", None),
        P("row", "col", None),
        P("row", "col"),
        P(("row", "col"), None),
        P(("row", "col"), None),
    )
    out_specs = (P(("row", "col"), None), P(("col", "row"), None), P(), P())
    return jax.shard_map(local, mesh=mesh, in_specs=in_specs, out_specs=out_specs, check_vma=False)
```

profile of v0, /device:TPU:1, one launch (start us, length us, event | category | flops | bytes accessed | tf_op | source)
XLA Modules:
  0.0 508.9 jit_solution(11679434189702534514)
XLA Ops:
  7.2 0.0 copy-start
  7.2 0.0 all-gather.3.cloned.1.call-start
  7.2 0.7 all-gather.3.cloned.1.call-update
  7.9 0.0 all-gather.5.cloned.1.call-start
  8.0 2.3 convert_reduce_fusion
  10.3 0.0 all-gather.5.cloned.1.call-update
  10.3 0.0 reduce-scatter.3.cloned.1.call-start
  11.0 0.7 compare_select_fusion.1
  11.7 0.7 compare_and_fusion.1
  12.4 54.7 %all-gather.3.cloned.1.call-done = bf16[8192,128]{1,0:T(8,128)(2,1)} async-done(((bf16[1024,128]{1,0:T(8,128)(2,1)}), bf16[8192,128]{1,0:T(8,128)(2,1)}) %all-gather.3.cloned.1.call-update) | async-done | bytes 2097168 | tf_op jit(solution)/shard_map/all_gather | solution.py:19
  67.1 10.3 %gather_fusion = bf16[256,128,128]{2,1,0:T(8,128)(2,1)} fusion(bf16[64,128,128]{2,1,0:T(8,128)(2,1)} %bitcast.30, s32[1024]{0:T(1024)S(1)} %pad_clamp_fusion.1), kind=kCustom, calls=%fused_computation | custom fusion | bytes 16778240 | tf_op jit(solution)/shard_map/jit(_take)/gather | solution.py:22
  77.4 13.9 %multiply_bitcast_fusion.1 = f32[256,128,128]{1,2,0:T(8,128)} fusion(bf16[1,1,256,128,128]{4,3,2,1,0:T(8,128)(2,1)} %param.12, f32[256]{0:T(256)S(1)} %compare_convert_fusion, bf16[256,128,128]{2,1,0:T(8,128)(2,1)} %gather_fusion, pred[256]{0:T(512)(128)(4,1)S(1)} %compare_and_fusion.1), kind=kOutput, calls=%fused_computation.6 | convolution fusion | flops 1082130432 | bytes 33555712 | tf_op jit(solution)/shard_map/kab,kbf->kaf/dot_general | solution.py:23
  91.3 17.6 %copy.16 = f32[256,128,128]{2,1,0:T(8,128)} copy(f32[256,128,128]{1,2,0:T(8,128)} %multiply_bitcast_fusion.1) | data formatting | bytes 33554432 | tf_op jit(solution)/shard_map/mul | solution.py:24
  108.8 0.0 copy-start.3
  108.8 4.3 broadcast_in_dim.27
  113.1 0.0 copy-done.3
  113.1 52.1 %scatter_fusion = f32[128,128,128]{2,1,0:T(8,128)} fusion(f32[128,128,128]{2,1,0:T(8,128)} %broadcast_in_dim.27, s32[256]{0:T(256)S(1)} %bitcast.31, f32[256,128,128]{2,1,0:T(8,128)} %copy.16), kind=kCustom, calls=%fused_computation.2 | custom fusion | flops 4194304 | bytes 50332672 | tf_op jit(solution)/shard_map/scatter-add | solution.py:25
  165.2 0.0 reduce-scatter.3.cloned.1.call-update
  165.2 0.2 reduce-scatter.5.cloned.1.call-start
  165.4 0.0 all-gather.5.cloned.1.call-done
  165.5 0.0 copy-done
  165.5 7.7 %convolution_convert_fusion = bf16[16384,128]{1,0:T(8,128)(2,1)} fusion(bf16[16384,256]{1,0:T(8,128)(2,1)} %all-gather.5.cloned.1.call-done, bf16[128,256]{1,0:T(8,128)(2,1)S(1)} %copy-done), kind=kOutput, calls=%fused_computation.4 | convolution fusion | flops 1075838976 | bytes 12648448 | tf_op jit(solution)/shard_map/dot_general | solution.py:38
  173.2 10.9 %gather_fusion.1 = bf16[256,128,128]{2,1,0:T(8,128)(2,1)} fusion(bf16[128,128,128]{2,1,0:T(8,128)(2,1)} %bitcast.29, s32[1024]{0:T(1024)S(1)} %pad_clamp_fusion), kind=kCustom, calls=%fused_computation.1 | custom fusion | bytes 16778240 | tf_op jit(solution)/shard_map/jit(_take)/gather | solution.py:42
  184.1 16.0 %multiply_bitcast_fusion = f32[256,128,128]{1,2,0:T(8,128)} fusion(bf16[1,1,256,128,128]{4,3,2,1,0:T(8,128)(2,1)} %param.12, bf16[256,128,128]{2,1,0:T(8,128)(2,1)} %gather_fusion.1, f32[256]{0:T(256)S(1)} %compare_convert_fusion, pred[256]{0:T(512)(128)(4,1)S(1)} %compare_and_fusion), kind=kOutput, calls=%fused_computation.5 | convolution fusion | flops 1082130432 | bytes 33555712 | tf_op jit(solution)/shard_map/kab,kaf->kbf/dot_general | solution.py:43
  200.0 0.0 copy-start.4
  200.0 17.6 %copy.18 = f32[256,128,128]{2,1,0:T(8,128)} copy(f32[256,128,128]{1,2,0:T(8,128)} %multiply_bitcast_fusion) | data formatting | bytes 33554432 | tf_op jit(solution)/shard_map/mul | solution.py:44
  217.6 2.4 broadcast_in_dim.30
  220.1 0.0 copy-done.4
  220.1 0.0 copy-start.1
  220.1 0.0 copy-start.2
  220.1 0.0 copy-start.5
  220.1 51.5 %scatter_fusion.1 = f32[64,128,128]{2,1,0:T(8,128)} fusion(f32[64,128,128]{2,1,0:T(8,128)} %broadcast_in_dim.30, s32[256]{0:T(256)S(1)} %bitcast.34, f32[256,128,128]{2,1,0:T(8,128)} %copy.18), kind=kCustom, calls=%fused_computation.3 | custom fusion | flops 4194304 | bytes 50332672 | tf_op jit(solution)/shard_map/scatter-add | solution.py:45
  271.6 0.0 reduce-scatter.5.cloned.1.call-update
  271.6 0.0 all-reduce.2.cloned.1.call-start
  271.7 69.1 %psum.15 = f32[256]{0:T(256)} all-reduce(f32[256]{0:T(256)S(1)} %get-tuple-element.4), channel_id=1, replica_groups=mesh['row'=8,'col'=16] {'row','col'}, use_global_device_ids=true, to_apply=%region_6.7 | all-reduce | flops 256 | bytes 2048 | tf_op jit(solution)/shard_map/psum | solution.py:36
  340.8 0.0 reduce-scatter.3.cloned.1.call-done
  340.8 0.0 copy-done.1
  340.8 2.0 fusion.10
  342.8 0.0 all-reduce.2.cloned.1.call-update
  342.8 0.0 copy-done.2
  342.8 0.0 copy-done.5
  342.8 2.1 fusion.9
  344.9 9.8 %reduce-scatter.5.cloned.1.call-done = f32[1024,128]{1,0:T(8,128)} async-done(((f32[8192,128]{1,0:T(8,128)}), f32[1024,128]{1,0:T(8,128)}) %reduce-scatter.5.cloned.1.call-update) | async-done | bytes 524304 | tf_op jit(solution)/shard_map/reduce_scatter | solution.py:48
  354.7 1.8 convert_element_type.38
  356.5 144.3 %all-reduce.2.cloned.1.call-done = f32[128,256]{1,0:T(8,128)} async-done(((f32[128,256]{1,0:T(8,128)}), f32[128,256]{1,0:T(8,128)}) %all-reduce.2.cloned.1.call-update) | async-done | bytes 131088 | tf_op jit(solution)/shard_map/psum | solution.py:36
  500.8 1.6 copy.25
  (5 shorter events, 0.0 us)
Async XLA Ops:
  7.2 158.3 %copy-start = (bf16[128,256]{1,0:T(8,128)(2,1)S(1)}, bf16[128,256]{1,0:T(8,128)(2,1)}, u32[]{:S(2)}) copy-start(bf16[128,256]{1,0:T(8,128)(2,1)} %param.10) | copy-start | bytes 196612
  7.2 59.9 %all-gather.3.cloned.1.call-start = ((), (), s32[]{:S(2)}) async-start(), calls=%async_computation.2 | async-start | bytes 2359296 | tf_op jit(solution)/shard_map/all_gather | solution.py:19
  7.9 157.6 %all-gather.5.cloned.1.call-start = ((), (), s32[]{:S(2)}) async-start(), calls=%async_computation.4 | async-start | bytes 8912896 | tf_op jit(solution)/shard_map/all_gather | solution.py:37
  10.3 330.5 %reduce-scatter.3.cloned.1.call-start = ((), (), s32[]{:S(2)}) async-start(), calls=%async_computation.3 | async-start | bytes 8912896 | tf_op jit(solution)/shard_map/reduce_scatter | solution.py:28
  108.8 4.3 copy-start.3
  165.2 189.5 %reduce-scatter.5.cloned.1.call-start = ((), (), s32[]{:S(2)}) async-start(), calls=%async_computation.5 | async-start | bytes 4718592 | tf_op jit(solution)/shard_map/reduce_scatter | solution.py:48
  200.0 20.0 %copy-start.4 = (s32[1,1,256]{2,1,0:T(1,128)S(1)}, s32[1,1,256]{2,1,0:T(1,128)}, u32[]{:S(2)}) copy-start(s32[1,1,256]{2,1,0:T(1,128)} %param.14) | copy-start | bytes 3076
  220.1 120.7 %copy-start.1 = (bf16[1024,256]{1,0:T(8,128)(2,1)S(1)}, bf16[1024,256]{1,0:T(8,128)(2,1)}, u32[]{:S(2)}) copy-start(bf16[1024,256]{1,0:T(8,128)(2,1)} %get-tuple-element.5) | copy-start | bytes 1572868
  220.1 122.7 %copy-start.2 = (s32[1024,256]{1,0:T(8,128)S(1)}, s32[1024,256]{1,0:T(8,128)}, u32[]{:S(2)}) copy-start(s32[1024,256]{1,0:T(8,128)} %param.17) | copy-start | bytes 3145732
  220.1 122.7 %copy-start.5 = (f32[256]{0:T(256)S(1)}, f32[256]{0:T(256)}, u32[]{:S(2)}) copy-start(f32[256]{0:T(256)} %param.11) | copy-start | bytes 3076
  271.6 229.2 %all-reduce.2.cloned.1.call-start = ((), (), s32[]{:S(2)}) async-start(), calls=%async_computation.6 | async-start | bytes 262144 | tf_op jit(solution)/shard_map/psum | solution.py:36
Sparse Core Ops, SparseCore 0:
  10.4 56.6 all-gather.2
  69.4 50.8 all-gather.4
  165.3 69.8 reduce-scatter.2
  271.7 82.9 reduce-scatter.4
  360.6 140.1 all-reduce.1
where the time goes:
time: 511 us; the launch traced here: 509 us
  waiting for transfers between devices  210 us (41%)
  other arithmetic  109 us (21%)
  blocking collectives  69.1 us (14%)
  local copies, waits for them, and re-layouts  64.7 us (13%)
  matrix products  41.6 us (8%)
  between operations  14.5 us (3%)
    psum x1, waiting for transfers between devices, local(): lax.psum((local_weight, local_bias), ('row', 'col'))  144 us
    psum x1, blocking collectives, local(): lax.psum((local_weight, local_bias), ('row', 'col'))  69.1 us
    all_gather x1, waiting for transfers between devices, local(): column_feats = lax.all_gather(features, 'row', axis=0, tiled=True)  54.7 us
    scatter-add x1, other arithmetic, local(): jax.ops.segment_sum(products, rows_index, num_segments=row_segments)  52.1 us
    scatter-add x1, other arithmetic, local(): jax.ops.segment_sum(backward, cols_index, num_segments=col_segments)  51.5 us
    mul x1, local copies, waits for them, and re-layouts, local(): backward = backward * alive_slots[:, None, None]  17.6 us
    mul x1, local copies, waits for them, and re-layouts, local(): products = products * alive_slots[:, None, None]  17.6 us
    dot_general x1, matrix products, local(): jnp.einsum('kab,kaf->kbf', blocks, picked_back, preferred_element_type=jn...  16 us
  transfers between devices with their start and end apart: 5, of which 3 were waited for; matrix products, arithmetic and copies ran while one was open for 42% of the time, Pallas kernels for 0%

commit v1 on v0

v1 whole, which is shorter than its diff:
```python
import functools

import jax
import jax.numpy as jnp
from jax import lax
from jax.experimental import pallas as pl
from jax.experimental.pallas import tpu as pltpu
from jax.sharding import PartitionSpec as P

F32 = jnp.float32
BF16 = jnp.bfloat16
MESH = pl.DeviceIdType.MESH
BLK = 128
SHARD = 8
HALF = 4


def plan_kernel(count_ref, rows_ref, cols_ref, idx_ref, flt_ref):
    n = rows_ref.shape[1]
    count = count_ref[0, 0]
    lane = lax.broadcasted_iota(jnp.int32, (n, n), 1)
    sub = lax.broadcasted_iota(jnp.int32, (n, n), 0)
    lane_f, sub_f = lane.astype(F32), sub.astype(F32)
    eye = lane == sub
    live_l, live_c = lane < count, sub < count
    row_l = jnp.broadcast_to(rows_ref[...].astype(F32), (n, n))
    col_l = jnp.broadcast_to(cols_ref[...].astype(F32), (n, n))
    zero = jnp.zeros((n, n), F32)
    row_c = jnp.broadcast_to(jnp.sum(jnp.where(eye, row_l, zero), axis=1, keepdims=True), (n, n))
    col_c = jnp.broadcast_to(jnp.sum(jnp.where(eye, col_l, zero), axis=1, keepdims=True), (n, n))
    idx_ref[...] = jnp.zeros_like(idx_ref)
    flt_ref[...] = jnp.zeros_like(flt_ref)
    one = jnp.ones((n, n), F32)
    for side, (major_l, major_c, minor_c) in enumerate(((row_l, row_c, col_c), (col_l, col_c, row_c))):
        far = jnp.full((n, n), 65536.0, F32)
        key_l = jnp.where(live_l, major_l * n, far) + lane_f
        key_c = jnp.where(live_c, major_c * n, far) + sub_f
        rank = jnp.sum(jnp.where(key_l < key_c, one, zero), axis=1, keepdims=True)
        hot = jnp.where(jnp.broadcast_to(rank, (n, n)) == lane_f, one, zero)
        same = jnp.where(major_l == major_c, one, zero) * jnp.where(lane < sub, one, zero) * jnp.where(live_l, one, zero)
        keep = jnp.where(jnp.sum(same, axis=1, keepdims=True) > 0.5, 1.0, 0.0)
        slot = jnp.sum(hot * sub_f, axis=0, keepdims=True)
        minor = jnp.sum(hot * minor_c, axis=0, keepdims=True)
        keep_sorted = jnp.sum(hot * keep, axis=0, keepdims=True)
        live_f = jnp.where(live_c, one, zero)
        upto = jnp.sum(jnp.where(major_c <= lane_f, live_f, zero), axis=0, keepdims=True)
        here = jnp.sum(jnp.where(major_c == lane_f, live_f, zero), axis=0, keepdims=True)
        idx_ref[3 * side : 3 * side + 1, :] = slot.astype(jnp.int32)
        idx_ref[3 * side + 1 : 3 * side + 2, :] = minor.astype(jnp.int32)
        idx_ref[3 * side + 2 : 3 * side + 3, :] = jnp.maximum(upto - 1.0, 0.0).astype(jnp.int32)
        flt_ref[2 * side : 2 * side + 1, :] = keep_sorted
        flt_ref[2 * side + 1 : 2 * side + 2, :] = jnp.where(here > 0.5, 1.0, 0.0)


class Lines:
    def __init__(self, send_sems, recv_sems):
        self.send_sems, self.recv_sems, self.used, self.sent = send_sems, recv_sems, 0, []

    def line(self):
        self.used += 1
        return self.used - 1

    def send(self, line, src, dst, device):
        copy = pltpu.make_async_remote_copy(
            src_ref=src, dst_ref=dst, send_sem=self.send_sems.at[line], recv_sem=self.recv_sems.at[line],
            device_id=device, device_id_type=MESH)
        copy.start()
        self.sent.append(copy)

    def wait(self, line, dst, device):
        pltpu.make_async_remote_copy(
            src_ref=dst, dst_ref=dst, send_sem=self.send_sems.at[line], recv_sem=self.recv_sems.at[line],
            device_id=device, device_id_type=MESH).wait_recv()

    def drain(self):
        for copy in self.sent:
            copy.wait_send()


N_LINES = 160


def layer_kernel(
    idx_ref, flt_ref, feat_ref, weight_ref, bias_ref, cot_ref, mask_ref, adj_ref,
    out_ref, gf_ref, gw_ref, gb_ref,
    adj, run, feats, proj, gpre, rsend, crecv, rown,
    zs1, zr1, zs2, zr2, zxs, zxr, ys1, yr1, ys2, yr2, yxs, yxr,
    agg, gsum, ar_core, ar_z, ar_y, ar_x, gall,
    send_sems, recv_sems, adj_sem):
    row, col = lax.axis_index("row"), lax.axis_index("col")
    xh, y = row // 4, row % 4
    xl, z, core = col // 8, (col // 2) % 4, col % 2
    lines = Lines(send_sems, recv_sems)

    def dev(xh=xh, y=y, xl=xl, z=z, core=core):
        return (xh * 4 + y, (xl * 4 + z) * 2 + core)

    def at_y(step):
        return dev(y=(y + step) % 4)

    def at_z(step):
        return dev(z=(z + step) % 4)

    pair_x = dev(xh=1 - xh)
    near_x = dev(xl=1 - xl)
    diag_x = dev(xh=1 - xh, xl=1 - xl)
    other = dev(core=1 - core)
    partners = [at_y(1), at_y(2), at_y(3), at_z(1), at_z(2), at_z(3), pair_x, near_x, diag_x, other]

    adj_copy = pltpu.make_async_copy(adj_ref, adj, adj_sem)
    adj_copy.start()

    barrier = pltpu.get_barrier_semaphore()
    for partner in partners:
        pl.semaphore_signal(barrier, inc=1, device_id=partner, device_id_type=MESH)
    pl.semaphore_wait(barrier, len(partners))

    def part(buf, shard, half):
        return buf.at[pl.ds(shard * SHARD + half * HALF, HALF)]

    class Gather:
        def __init__(self, buf, own, shard, pos, pair, ring, mate):
            self.buf, self.own, self.shard, self.pos, self.pair, self.ring, self.mate = buf, own, shard, pos, pair, ring, mate
            self.l0 = [lines.line() for _ in range(2)]
            self.l1 = [[lines.line() for _ in range(2)] for _ in range(2)]
            self.l2 = [lines.line() for _ in range(2)]
            self.l3 = [[lines.line() for _ in range(2)] for _ in range(2)]
            self.l4 = [lines.line() for _ in range(2)]

        def place(self, pair_step, step, half):
            pair = self.pair if pair_step == 0 else 1 - self.pair
            return part(self.buf, self.shard(pair, (self.pos + step) % 4), half)

        def begin(self):
            for half in range(2):
                for d in range(2):
                    h = half if d == 0 else 1 - half
                    lines.send(self.l1[d][h], self.own(h), self.place(0, 0, h), self.ring(1 - 2 * d))
            for half in range(2):
                lines.send(self.l0[half], self.own(half), self.place(0, 0, half), self.mate)

        def got_mate(self, h):
            lines.wait(self.l0[h], self.place(1, 0, h), self.mate)
            return self.place(1, 0, h)

        def pass_mate(self, h):
            for d in range(2):
                lines.send(self.l3[d][h], self.place(1, 0, h), self.place(1, 0, h), self.ring(1 - 2 * d))

        def got_ring(self, kind, d, h):
            step = 2 * d - 1
            table = self.l1 if kind == 0 else self.l3
            place = self.place(kind, step, h)
            lines.wait(table[d][h], place, self.ring(step))
            return place

        def pass_ring(self, kind, d):
            step = 2 * d - 1
            table = self.l2 if kind == 0 else self.l4
            place = self.place(kind, step, d)
            lines.send(table[d], place, place, self.ring(-step))

        def got_far(self, kind, d):
            step = 2 * d - 1
            table = self.l2 if kind == 0 else self.l4
            place = self.place(kind, 2, d)
            lines.wait(table[d], place, self.ring(step))
            return place

    rows_g = Gather(feats, lambda h: feat_ref.at[pl.ds(h * HALF, HALF)],
                    lambda pair, pos: pair * 4 + pos, y, xh, at_y, pair_x)
    rows_g.begin()

    gb_ref[...] = jnp.zeros_like(gb_ref)

    def project(b, _):
        nodes = pl.ds(pl.multiple_of(b * BLK, BLK), BLK)
        grad = cot_ref[nodes, :].astype(F32) * mask_ref[nodes, :].astype(F32)
        grad16 = grad.astype(BF16)
        gpre[nodes, :] = grad16
        gb_ref[...] += jnp.sum(grad16.astype(F32), axis=0, keepdims=True)
        turned = lax.dot_general(weight_ref[...], grad16, (((1,), (1,)), ((), ())), preferred_element_type=F32)
        proj[col * SHARD + b] = turned.astype(BF16)
        return 0

    lax.fori_loop(0, SHARD, project, 0)
    cols_g = Gather(proj, lambda h: part(proj, col, h),
                    lambda pair, pos: (pair * 4 + pos) * 2 + core, z, xl, at_z, near_x)
    cols_g.begin()

    across = []

    def cross(pair_step, step, h):
        line = lines.line()
        place = cols_g.place(pair_step, step, h)
        lines.send(line, place, place, other)
        pair = xl if pair_step == 0 else 1 - xl
        there = part(proj, (pair * 4 + (z + step) % 4) * 2 + 1 - core, h)
        across.append((line, there))

    feats[pl.ds(row * SHARD, SHARD)] = feat_ref[...]

    cross(0, 0, 0)
    cross(0, 0, 1)
    for d in range(2):
        rows_g.got_ring(0, d, d)
        rows_g.pass_ring(0, d)
    for h in range(2):
        rows_g.got_mate(h)
        rows_g.pass_mate(h)
    for d in range(2):
        cols_g.got_ring(0, d, d)
        cols_g.pass_ring(0, d)
    for h in range(2):
        cols_g.got_mate(h)
        cols_g.pass_mate(h)
    for d in range(2):
        cross(0, 2 * d - 1, d)
    for h in range(2):
        cross(1, 0, h)
    for d in range(2):
        cols_g.got_ring(0, d, 1 - d)
        cross(0, 2 * d - 1, 1 - d)
    for d in range(2):
        rows_g.got_ring(1, d, d)
        rows_g.pass_ring(1, d)
    for d in range(2):
        cols_g.got_ring(1, d, d)
        cols_g.pass_ring(1, d)
        cross(1, 2 * d - 1, d)
    for d in range(2):
        cols_g.got_far(0, d)
        cross(0, 2, d)
    for d in range(2):
        cols_g.got_ring(1, d, 1 - d)
        cross(1, 2 * d - 1, 1 - d)
    for d in range(2):
        rows_g.got_ring(0, d, 1 - d)
        rows_g.got_far(0, d)
        rows_g.got_ring(1, d, 1 - d)
    for d in range(2):
        rows_g.got_far(1, d)
    for d in range(2):
        cols_g.got_far(1, d)
        cross(1, 2, d)
    adj_copy.wait()

    slots = adj.shape[0]

    def forward(p, total):
        total = total * flt_ref[0, p] + jnp.dot(adj[idx_ref[0, p]], feats[idx_ref[1, p]], preferred_element_type=F32)
        run[p] = total
        return total

    lax.fori_loop(0, slots, forward, jnp.zeros((BLK, BLK), F32), unroll=8)

    def row_block(b):
        return run[idx_ref[2, b]] * flt_ref[1, b]

    order = [(pair_step, step) for step in (2, 1, -1, 0) for pair_step in (1, 0)]

    def spot(pair, pos, step):
        return pair * 4 + (pos + step) % 4

    core_lines = {}
    for pair_step, step in order:
        q = spot(1 - xl if pair_step else xl, z, step)

        def fill(b, _, q=q):
            rsend[q * SHARD + b] = row_block((q * 2 + 1 - core) * SHARD + b).astype(BF16)
            return 0

        lax.fori_loop(0, SHARD, fill, 0)
        line = core_lines[pair_step, step] = lines.line()
        place = pl.ds(q * SHARD, SHARD)
        lines.send(line, rsend.at[place], crecv.at[place], other)

    def add_core(pair_step, step):
        q = spot(1 - xl if pair_step else xl, z, step)
        lines.wait(core_lines[pair_step, step], crecv.at[pl.ds(q * SHARD, SHARD)], other)

        def fill(b, _):
            rown[q * SHARD + b] = row_block((q * 2 + core) * SHARD + b) + crecv[q * SHARD + b].astype(F32)
            return 0

        lax.fori_loop(0, SHARD, fill, 0)

    class Scatter:
        def __init__(self, s1, r1, s2, r2, xs, xr, term, ring, mate):
            self.s1, self.r1, self.s2, self.r2, self.xs, self.xr = s1, r1, s2, r2, xs, xr
            self.term, self.ring, self.mate = term, ring, mate
            self.l1 = [[lines.line() for _ in range(2)] for _ in range(2)]
            self.l2 = [[[lines.line() for _ in range(2)] for _ in range(2)] for _ in range(2)]
            self.lx = [lines.line() for _ in range(2)]

        def far(self, pair_step):
            for d in range(2):
                def fill(b, _, d=d):
                    b = d * HALF + b
                    self.s1[pair_step * SHARD + b] = self.term(pair_step, 2, b).astype(BF16)
                    return 0

                lax.fori_loop(0, HALF, fill, 0)
                place = pl.ds(pair_step * SHARD + d * HALF, HALF)
                lines.send(self.l1[pair_step][d], self.s1.at[place], self.r1.at[place], self.ring(1 - 2 * d))

        def near(self, pair_step, d, late):
            h = d if late else 1 - d
            base = (pair_step * 2 + d) * SHARD + h * HALF
            if late:
                place = pl.ds(pair_step * SHARD + d * HALF, HALF)
                lines.wait(self.l1[pair_step][d], self.r1.at[place], self.ring(2 * d - 1))

            def fill(b, _):
                value = self.term(pair_step, 1 - 2 * d, h * HALF + b)
                if late:
                    value = value + self.r1[pair_step * SHARD + d * HALF + b].astype(F32)
                self.s2[base + b] = value.astype(BF16)
                return 0

            lax.fori_loop(0, HALF, fill, 0)
            place = pl.ds(base, HALF)
            lines.send(self.l2[pair_step][d][h], self.s2.at[place], self.r2.at[place], self.ring(1 - 2 * d))

        def wait_near(self, pair_step, h):
            for d in range(2):
                place = pl.ds((pair_step * 2 + d) * SHARD + h * HALF, HALF)
                lines.wait(self.l2[pair_step][d][h], self.r2.at[place], self.ring(2 * d - 1))

        def total(self, pair_step, b):
            base = pair_step * 2 * SHARD + b
            return (self.term(pair_step, 0, b) + self.r2[base].astype(F32)) + self.r2[base + SHARD].astype(F32)

        def swap(self, h):
            self.wait_near(1, h)

            def fill(b, _):
                self.xs[h * HALF + b] = self.total(1, h * HALF + b).astype(BF16)
                return 0

            lax.fori_loop(0, HALF, fill, 0)
            place = pl.ds(h * HALF, HALF)
            lines.send(self.lx[h], self.xs.at[place], self.xr.at[place], self.mate)

        def finish(self, h, use):
            self.wait_near(0, h)
            lines.wait(self.lx[h], self.xr.at[pl.ds(h * HALF, HALF)], self.mate)

            def body(b, _):
                b = h * HALF + b
                use(b, self.total(0, b) + self.xr[b].astype(F32))
                return 0

            lax.fori_loop(0, HALF, body, 0)

    def row_term(pair_step, step, b):
        return rown[spot(1 - xl if pair_step else xl, z, step) * SHARD + b]

    rows_s = Scatter(zs1, zr1, zs2, zr2, zxs, zxr, row_term, at_z, near_x)
    for pair_step in (1, 0):
        add_core(pair_step, 2)
        rows_s.far(pair_step)
    for pair_step in (1, 0):
        for d in range(2):
            add_core(pair_step, 1 - 2 * d)
            rows_s.near(pair_step, d, False)
    for pair_step in (1, 0):
        add_core(pair_step, 0)

    for line, there in across:
        lines.wait(line, there, other)

    def backward(p, total):
        total = total * flt_ref[2, p] + jnp.dot(proj[idx_ref[4, p]], adj[idx_ref[3, p]], preferred_element_type=F32)
        run[p] = total
        return total

    lax.fori_loop(0, slots, backward, jnp.zeros((BLK, BLK), F32), unroll=8)

    def col_term(pair_step, step, b):
        at = spot(1 - xh if pair_step else xh, y, step) * SHARD + b
        return run[idx_ref[5, at]] * flt_ref[3, at]

    cols_s = Scatter(ys1, yr1, ys2, yr2, yxs, yxr, col_term, at_y, pair_x)
    for pair_step in (1, 0):
        cols_s.far(pair_step)
    for pair_step in (1, 0):
        for d in range(2):
            cols_s.near(pair_step, d, False)
    for pair_step in (1, 0):
        for d in range(2):
            rows_s.near(pair_step, d, True)
    for h in range(2):
        rows_s.swap(h)
    for pair_step in (1, 0):
        for d in range(2):
            cols_s.near(pair_step, d, True)

    def layer(b, value):
        nodes = pl.ds(pl.multiple_of(b * BLK, BLK), BLK)
        sums = value.astype(BF16)
        agg[b] = sums
        pre = jnp.dot(sums, weight_ref[...], preferred_element_type=F32) + bias_ref[...]
        out_ref[nodes, :] = (pre * mask_ref[nodes, :].astype(F32)).astype(BF16)

    for h in range(2):
        rows_s.finish(h, layer)

    def weight_term(b, total):
        nodes = pl.ds(pl.multiple_of(b * BLK, BLK), BLK)
        return total + lax.dot_general(agg[b], gpre[nodes, :], (((0,), (0,)), ((), ())), preferred_element_type=F32)

    gw_ref[...] = lax.fori_loop(0, SHARD, weight_term, jnp.zeros(gw_ref.shape, F32))

    pieces = gsum.shape[0]
    depth = gw_ref.shape[0] // pieces
    for n in range(pieces):
        gsum[n, pl.ds(0, depth), :] = gw_ref[pl.ds(n * depth, depth), :]
        gsum[n, pl.ds(depth, 8), :] = jnp.broadcast_to(gb_ref[...], (8, gb_ref.shape[1]))
    line = lines.line()
    lines.send(line, gsum.at[pl.ds((1 - core) * 4, 4)], ar_core, other)
    for h in range(2):
        cols_s.swap(h)
    lines.wait(line, ar_core, other)
    for n in range(4):
        ar_core[n] = ar_core[n] + gsum[core * 4 + n]

    z_lines = [lines.line() for _ in range(3)]
    for step in (2, 1, 3):
        lines.send(z_lines[step - 1], ar_core.at[(z + step) % 4], ar_z.at[step], at_z(step))
    ar_z[0] = ar_core[z]
    for step in (1, 2, 3):
        lines.wait(z_lines[step - 1], ar_z.at[step], at_z(4 - step))
    ar_y[y] = (ar_z[0] + ar_z[1]) + (ar_z[2] + ar_z[3])
    y_lines = [lines.line() for _ in range(3)]
    for step in (2, 1, 3):
        lines.send(y_lines[step - 1], ar_y.at[y], ar_y.at[y], at_y(step))
    for step in (1, 2, 3):
        lines.wait(y_lines[step - 1], ar_y.at[(y + 4 - step) % 4], at_y(4 - step))
    x = xh * 2 + xl
    ar_x[x] = (ar_y[0] + ar_y[1]) + (ar_y[2] + ar_y[3])
    x_mates = [(near_x, xh * 2 + 1 - xl), (pair_x, (1 - xh) * 2 + xl), (diag_x, (1 - xh) * 2 + 1 - xl)]
    x_lines = [lines.line() for _ in range(3)]
    for line, (mate, _) in zip(x_lines, x_mates):
        lines.send(line, ar_x.at[x], ar_x.at[x], mate)
    for line, (mate, place) in zip(x_lines, x_mates):
        lines.wait(line, ar_x.at[place], mate)
    mine = core * 4 + z
    gall[mine] = (ar_x[0] + ar_x[1]) + (ar_x[2] + ar_x[3])
    e_lines = [lines.line() for _ in range(3)]
    for step in (2, 1, 3):
        lines.send(e_lines[step - 1], gall.at[mine], gall.at[mine], at_z(step))
    for step in (1, 2, 3):
        lines.wait(e_lines[step - 1], gall.at[core * 4 + (z + 4 - step) % 4], at_z(4 - step))
    line = lines.line()
    lines.send(line, gall.at[pl.ds(core * 4, 4)], gall.at[pl.ds(core * 4, 4)], other)

    def store(b, value):
        gf_ref[b] = jnp.transpose(value).astype(BF16)

    for h in range(2):
        cols_s.finish(h, store)

    lines.wait(line, gall.at[pl.ds((1 - core) * 4, 4)], other)
    for n in range(pieces):
        gw_ref[pl.ds(n * depth, depth), :] = gall[n, pl.ds(0, depth), :]
    gb_ref[...] = gall[0, pl.ds(depth, 1), :]
    lines.drain()
    assert lines.used <= N_LINES


def local(features, weight, bias, adjacency, block_rows, block_cols, block_count, cotangent, relu_mask):
    slots = adjacency.shape[2]
    vmem, smem, hbm = (pl.BlockSpec(memory_space=m) for m in (pltpu.VMEM, pltpu.SMEM, pl.ANY))
    idx, flt = pl.pallas_call(
        plan_kernel,
        out_shape=(jax.ShapeDtypeStruct((8, slots), jnp.int32), jax.ShapeDtypeStruct((8, slots), F32)),
        in_specs=[smem, vmem, vmem],
        out_specs=(vmem, vmem),
        name="plan",
    )(block_count, block_rows[0], block_cols[0])
    hid = weight.shape[1]

    def blocks(n, dtype=BF16):
        return pltpu.VMEM((n, BLK, BLK), dtype)

    scratch = [
        blocks(slots), blocks(slots, F32), blocks(64), blocks(128), pltpu.VMEM((1024, hid), BF16),
        blocks(64), blocks(64), blocks(64, F32)]
    for _ in range(2):
        scratch += [blocks(16), blocks(16), blocks(32), blocks(32), blocks(8), blocks(8)]
    piece = (24, hid)
    scratch += [blocks(8), pltpu.VMEM((8,) + piece, F32)]
    scratch += [pltpu.VMEM((4,) + piece, F32) for _ in range(4)] + [pltpu.VMEM((8,) + piece, F32)]
    scratch += [pltpu.SemaphoreType.DMA((N_LINES,)), pltpu.SemaphoreType.DMA((N_LINES,)), pltpu.SemaphoreType.DMA]
    out, gf, gw, gb = pl.pallas_call(
        layer_kernel,
        out_shape=(
            jax.ShapeDtypeStruct((1024, hid), BF16),
            jax.ShapeDtypeStruct((SHARD, BLK, BLK), BF16),
            jax.ShapeDtypeStruct(weight.shape, F32),
            jax.ShapeDtypeStruct((1, hid), F32),
        ),
        in_specs=[smem, smem, vmem, vmem, vmem, vmem, vmem, hbm],
        out_specs=(vmem, vmem, vmem, vmem),
        scratch_shapes=scratch,
        compiler_params=pltpu.CompilerParams(collective_id=0, has_side_effects=True, vmem_limit_bytes=60 * 2**20),
        name="layer",
    )(idx, flt, features.reshape(SHARD, BLK, BLK), weight, bias.reshape(1, hid), cotangent, relu_mask,
      adjacency.reshape(slots, BLK, BLK))
    return out, gf.reshape(1024, BLK), gw, gb.reshape(hid)


def solution(mesh):
    in_specs = (
        P(("col", "row"), None),
        P(),
        P(),
        P("row", "col", None, None, None),
        P("row", "col", None),
        P("row", "col", None),
        P("row", "col"),
        P(("row", "col"), None),
        P(("row", "col"), None),
    )
    out_specs = (P(("row", "col"), None), P(("col", "row"), None), P(), P())
    return jax.shard_map(local, mesh=mesh, in_specs=in_specs, out_specs=out_specs, check_vma=False)
```

time: 511 us -> 97.1 us (0.19)
  waiting for transfers between devices: 210 us -> 0 us
  other arithmetic: 109 us -> 0 us
  Pallas kernels: 0 us -> 89.2 us
  blocking collectives: 69.1 us -> 0 us
  local copies, waits for them, and re-layouts: 64.7 us -> 6.33 us
  matrix products: 41.6 us -> 0 us
  between operations: 14.5 us -> 1.29 us
    psum x1 -> x0, waiting for transfers between devices: 144 us -> none  [local(): lax.psum((local_weight, local_bias), ('row', 'col'))]
    scatter-add x2 -> x0, other arithmetic: 104 us -> none  [the longest x1 52.1 us: local(): jax.ops.segment_sum(products, rows_index, num_segments=row_segments)]
    pallas_call x0 -> x2, Pallas kernels: none -> 89.2 us  [the longest x1 87.4 us: local(): pl.pallas_call(layer_kernel, out_shape=(jax.ShapeDtypeStruct((1024, hid),...]
    psum x1 -> x0, blocking collectives: 69.1 us -> none  [local(): lax.psum((local_weight, local_bias), ('row', 'col'))]
    all_gather x2 -> x0, waiting for transfers between devices: 54.7 us -> none  [the longest x1 54.7 us: local(): column_feats = lax.all_gather(features, 'row', axis=0, tiled=True)]
    dot_general x5 -> x0, matrix products: 41.6 us -> none  [the longest x1 16 us: local(): jnp.einsum('kab,kaf->kbf', blocks, picked_back, preferred_element_type=jn...]
    mul x2 -> x0, local copies, waits for them, and re-layouts: 35.2 us -> none  [the longest x1 17.6 us: local(): backward = backward * alive_slots[:, None, None]]
    gather x2 -> x0, local copies, waits for them, and re-layouts: 21.2 us -> none  [the longest x1 10.9 us: local(): picked_back = jnp.take(proj_blocks, rows_index, axis=0)]
  transfers between devices with their start and end apart: 5 -> 0, of which waited for: 3 -> 0; matrix products, arithmetic and copies ran while one was open for 42% -> 0% of each run, Pallas kernels for 0% -> 0%
where the time goes in v1:
time: 97.1 us; the launch traced here: 96.8 us
  Pallas kernels  89.2 us (92%)
  local copies, waits for them, and re-layouts  6.33 us (7%)
  between operations  1.29 us (1%)
    pallas_call x1, Pallas kernels, local(): pl.pallas_call(layer_kernel, out_shape=(jax.ShapeDtypeStruct((1024, hid),...  87.4 us
    unnamed x4, local copies, waits for them, and re-layouts  6.33 us

profile of v1, /device:TPU:1, one launch (start us, length us, event | category | flops | bytes accessed | tf_op | source)
XLA Modules:
  0.0 96.8 jit_solution(4351580655344154688)
XLA Ops:
  1.3 1.8 %plan.1 = (s32[8,256]{1,0:T(8,128)}, f32[8,256]{1,0:T(8,128)}) custom-call(s32[1,1]{1,0:T(1,128)S(6)} %copy.17.count_ref, s32[1,256]{1,0:T(1,128)} %bitcast.10, s32[1,256]{1,0:T(1,128)} %bitcast.11), custom_call_target="tpu_custom_call" | custom-call | tf_op jit(solution)/shard_map/plan/pallas_call | solution.py:475
  3.1 87.4 %layer.1 = (bf16[1024,256]{1,0:T(8,128)(2,1)}, bf16[8,128,128]{2,1,0:T(8,128)(2,1)}, f32[128,256]{1,0:T(8,128)}, f32[1,256]{1,0:T(1,128)}) custom-call(s32[8,256]{1,0:T(8,128)} %get-tuple-element.10.idx_ref, f32[8,256]{1,0:T(8,128)} %get-tuple-element.11.flt_ref, bf16[8,128,128]{2,1,0:T(8,128)(2,1)} %bitcast.8, bf16[128,256]{1,0:T(8,128)(2,1)} %weight_ref.1, ...), custom_call_target="tpu_custom_call" | custom-call | tf_op jit(solution)/shard_map/layer/pallas_call | solution.py:496
  90.5 1.9 %copy.18 = bf16[1024,256]{1,0:T(8,128)(2,1)} copy(bf16[1024,256]{1,0:T(8,128)(2,1)} %get-tuple-element.20) | data formatting | bytes 1048576
  92.3 1.7 %copy.19 = bf16[1024,128]{1,0:T(8,128)(2,1)} copy(bf16[1024,128]{1,0:T(8,128)(2,1)} %bitcast.9) | data formatting | bytes 524288
  94.0 1.6 %copy.20 = f32[128,256]{1,0:T(8,128)} copy(f32[128,256]{1,0:T(8,128)} %get-tuple-element.22) | data formatting | bytes 262144
  95.6 1.2 %copy.21 = f32[256]{0:T(256)} copy(f32[256]{0:T(256)} %bitcast.12) | data formatting | bytes 2048

commit v2 on v1

--- a/solution.py
+++ b/solution.py
@@ -52,6 +52,12 @@
         flt_ref[2 * side + 1 : 2 * side + 2, :] = jnp.where(here > 0.5, 1.0, 0.0)
 
 
+def hand_on_kernel(*refs):
+    half = len(refs) // 2
+    for source, target in zip(refs[:half], refs[half:]):
+        target[...] = source[...]
+
+
 class Lines:
     def __init__(self, send_sems, recv_sems):
         self.send_sems, self.recv_sems, self.used, self.sent = send_sems, recv_sems, 0, []
@@ -81,12 +87,12 @@
 
 
 def layer_kernel(
-    idx_ref, flt_ref, feat_ref, weight_ref, bias_ref, cot_ref, mask_ref, adj_ref,
+    idx_ref, flt_ref, feat_ref, weight_ref, bias_ref, cot_hbm, mask_hbm, adj_ref,
     out_ref, gf_ref, gw_ref, gb_ref,
-    adj, run, feats, proj, gpre, rsend, crecv, rown,
+    cot_ref, mask_ref, adj, run, feats, proj, gpre, rsend, crecv, rown,
     zs1, zr1, zs2, zr2, zxs, zxr, ys1, yr1, ys2, yr2, yxs, yxr,
-    agg, gsum, ar_core, ar_z, ar_y, ar_x, gall,
-    send_sems, recv_sems, adj_sem):
+    agg, gsum, ar_col, ar_row, gall, bias_own, bias_col, bias_row,
+    send_sems, recv_sems, in_sems):
     row, col = lax.axis_index("row"), lax.axis_index("col")
     xh, y = row // 4, row % 4
     xl, z, core = col // 8, (col // 2) % 4, col % 2
@@ -103,75 +109,31 @@
 
     pair_x = dev(xh=1 - xh)
     near_x = dev(xl=1 - xl)
-    diag_x = dev(xh=1 - xh, xl=1 - xl)
     other = dev(core=1 - core)
-    partners = [at_y(1), at_y(2), at_y(3), at_z(1), at_z(2), at_z(3), pair_x, near_x, diag_x, other]
-
-    adj_copy = pltpu.make_async_copy(adj_ref, adj, adj_sem)
-    adj_copy.start()
+    col_mates, row_mates = [], []
+    for flip in (1, 0):
+        for step in (2, 1, 3, 0):
+            for turn in (1, 0):
+                if flip or step or turn:
+                    to_xl, to_z, to_core = (xl + flip) % 2, (z + step) % 4, (core + turn) % 2
+                    col_mates.append((dev(xl=to_xl, z=to_z, core=to_core), (to_xl * 4 + to_z) * 2 + to_core))
+            if flip or step:
+                to_xh, to_y = (xh + flip) % 2, (y + step) % 4
+                row_mates.append((dev(xh=to_xh, y=to_y), to_xh * 4 + to_y))
+    partners = [mate for mate, _ in row_mates + col_mates]
+    cot_copy = pltpu.make_async_copy(cot_hbm, cot_ref, in_sems.at[0])
+    mask_copy = pltpu.make_async_copy(mask_hbm, mask_ref, in_sems.at[1])
+    adj_copy = pltpu.make_async_copy(adj_ref, adj, in_sems.at[2])
+    for copy in (cot_copy, mask_copy, adj_copy):
+        copy.start()
 
     barrier = pltpu.get_barrier_semaphore()
     for partner in partners:
         pl.semaphore_signal(barrier, inc=1, device_id=partner, device_id_type=MESH)
-    pl.semaphore_wait(barrier, len(partners))
-
-    def part(buf, shard, half):
-        return buf.at[pl.ds(shard * SHARD + half * HALF, HALF)]
-
-    class Gather:
-        def __init__(self, buf, own, shard, pos, pair, ring, mate):
-            self.buf, self.own, self.shard, self.pos, self.pair, self.ring, self.mate = buf, own, shard, pos, pair, ring, mate
-            self.l0 = [lines.line() for _ in range(2)]
-            self.l1 = [[lines.line() for _ in range(2)] for _ in range(2)]
-            self.l2 = [lines.line() for _ in range(2)]
-            self.l3 = [[lines.line() for _ in range(2)] for _ in range(2)]
-            self.l4 = [lines.line() for _ in range(2)]
-
-        def place(self, pair_step, step, half):
-            pair = self.pair if pair_step == 0 else 1 - self.pair
-            return part(self.buf, self.shard(pair, (self.pos + step) % 4), half)
-
-        def begin(self):
-            for half in range(2):
-                for d in range(2):
-                    h = half if d == 0 else 1 - half
-                    lines.send(self.l1[d][h], self.own(h), self.place(0, 0, h), self.ring(1 - 2 * d))
-            for half in range(2):
-                lines.send(self.l0[half], self.own(half), self.place(0, 0, half), self.mate)
-
-        def got_mate(self, h):
-            lines.wait(self.l0[h], self.place(1, 0, h), self.mate)
-            return self.place(1, 0, h)
-
-        def pass_mate(self, h):
-            for d in range(2):
-                lines.send(self.l3[d][h], self.place(1, 0, h), self.place(1, 0, h), self.ring(1 - 2 * d))
-
-        def got_ring(self, kind, d, h):
-            step = 2 * d - 1
-            table = self.l1 if kind == 0 else self.l3
-            place = self.place(kind, step, h)
-            lines.wait(table[d][h], place, self.ring(step))
-            return place
-
-        def pass_ring(self, kind, d):
-            step = 2 * d - 1
-            table = self.l2 if kind == 0 else self.l4
-            place = self.place(kind, step, d)
-            lines.send(table[d], place, place, self.ring(-step))
-
-        def got_far(self, kind, d):
-            step = 2 * d - 1
-            table = self.l2 if kind == 0 else self.l4
-            place = self.place(kind, 2, d)
-            lines.wait(table[d], place, self.ring(step))
-            return place
-
-    rows_g = Gather(feats, lambda h: feat_ref.at[pl.ds(h * HALF, HALF)],
-                    lambda pair, pos: pair * 4 + pos, y, xh, at_y, pair_x)
-    rows_g.begin()
 
     gb_ref[...] = jnp.zeros_like(gb_ref)
+    cot_copy.wait()
+    mask_copy.wait()
 
     def project(b, _):
         nodes = pl.ds(pl.multiple_of(b * BLK, BLK), BLK)
@@ -183,7 +145,65 @@
         proj[col * SHARD + b] = turned.astype(BF16)
         return 0
 
-    lax.fori_loop(0, SHARD, project, 0)
+    lax.fori_loop(0, SHARD, project, 0, unroll=SHARD)
+    pl.semaphore_wait(barrier, len(partners))
+
+    def part(buf, shard, half):
+        return buf.at[pl.ds(shard * SHARD + half * HALF, HALF)]
+
+    class Gather:
+        def __init__(self, buf, own, shard, pos, pair, ring, mate):
+            self.buf, self.own, self.shard, self.pos, self.pair, self.ring, self.mate = buf, own, shard, pos, pair, ring, mate
+            self.l0 = [lines.line() for _ in range(2)]
+            self.l1 = [[lines.line() for _ in range(2)] for _ in range(2)]
+            self.l2 = [lines.line() for _ in range(2)]
+            self.l3 = [[lines.line() for _ in range(2)] for _ in range(2)]
+            self.l4 = [lines.line() for _ in range(2)]
+
+        def place(self, pair_step, step, half):
+            pair = self.pair if pair_step == 0 else 1 - self.pair
+            return part(self.buf, self.shard(pair, (self.pos + step) % 4), half)
+
+        def begin(self):
+            for half in range(2):
+                for d in range(2):
+                    h = half if d == 0 else 1 - half
+                    lines.send(self.l1[d][h], self.own(h), self.place(0, 0, h), self.ring(1 - 2 * d))
+                lines.send(self.l0[half], self.own(half), self.place(0, 0, half), self.mate)
+
+        def got_mate(self, h):
+            lines.wait(self.l0[h], self.place(1, 0, h), self.mate)
+            return self.place(1, 0, h)
+
+        def pass_mate(self, late, cross=True):
+            for d in range(2):
+                h = (1 - d if late else d) if cross else late
+                lines.send(self.l3[d][h], self.place(1, 0, h), self.place(1, 0, h), self.ring(1 - 2 * d))
+
+        def got_ring(self, kind, d, h):
+            step = 2 * d - 1
+            table = self.l1 if kind == 0 else self.l3
+            place = self.place(kind, step, h)
+            lines.wait(table[d][h], place, self.ring(step))
+            return place
+
+        def pass_ring(self, kind, d):
+            step = 2 * d - 1
+            table = self.l2 if kind == 0 else self.l4
+            place = self.place(kind, step, d)
+            lines.send(table[d], place, place, self.ring(-step))
+
+        def got_far(self, kind, d):
+            step = 2 * d - 1
+            table = self.l2 if kind == 0 else self.l4
+            place = self.place(kind, 2, d)
+            lines.wait(table[d], place, self.ring(step))
+            return place
+
+    rows_g = Gather(feats, lambda h: feat_ref.at[pl.ds(h * HALF, HALF)],
+                    lambda pair, pos: pair * 4 + pos, y, xh, at_y, pair_x)
+    rows_g.begin()
+
     cols_g = Gather(proj, lambda h: part(proj, col, h),
                     lambda pair, pos: (pair * 4 + pos) * 2 + core, z, xl, at_z, near_x)
     cols_g.begin()
@@ -205,45 +225,59 @@
     for d in range(2):
         rows_g.got_ring(0, d, d)
         rows_g.pass_ring(0, d)
-    for h in range(2):
-        rows_g.got_mate(h)
-        rows_g.pass_mate(h)
     for d in range(2):
         cols_g.got_ring(0, d, d)
         cols_g.pass_ring(0, d)
     for h in range(2):
+        rows_g.got_mate(h)
+    for late in range(2):
+        rows_g.pass_mate(late)
+    for h in range(2):
         cols_g.got_mate(h)
-        cols_g.pass_mate(h)
+        cols_g.pass_mate(h, False)
     for d in range(2):
         cross(0, 2 * d - 1, d)
-    for h in range(2):
-        cross(1, 0, h)
+        cross(1, 0, d)
     for d in range(2):
         cols_g.got_ring(0, d, 1 - d)
         cross(0, 2 * d - 1, 1 - d)
     for d in range(2):
         rows_g.got_ring(1, d, d)
         rows_g.pass_ring(1, d)
+    for d in range(2):
+        cols_g.got_far(0, d)
+        cross(0, 2, d)
     for d in range(2):
         cols_g.got_ring(1, d, d)
         cols_g.pass_ring(1, d)
         cross(1, 2 * d - 1, d)
     for d in range(2):
-        cols_g.got_far(0, d)
-        cross(0, 2, d)
-    for d in range(2):
-        cols_g.got_ring(1, d, 1 - d)
-        cross(1, 2 * d - 1, 1 - d)
-    for d in range(2):
         rows_g.got_ring(0, d, 1 - d)
         rows_g.got_far(0, d)
         rows_g.got_ring(1, d, 1 - d)
     for d in range(2):
         rows_g.got_far(1, d)
-    for d in range(2):
-        cols_g.got_far(1, d)
-        cross(1, 2, d)
     adj_copy.wait()
+
+    def spread(mates, source, target, place):
+        used = [lines.line() for _ in mates]
+        for line, (mate, theirs) in zip(used, mates):
+            lines.send(line, source(theirs), target.at[place], mate)
+        return used
+
+    def collect(mates, used, target):
+        for line, (mate, theirs) in zip(used, mates):
+            lines.wait(line, target.at[theirs], mate)
+
+    def added(ref):
+        total = ref[0]
+        for n in range(1, ref.shape[0]):
+            total = total + ref[n]
+        return total
+
+    bias_own[...] = jnp.broadcast_to(gb_ref[...], bias_own.shape)
+    bias_col[col] = bias_own[...]
+    bias_lines = spread(col_mates, lambda theirs: bias_own, bias_col, col)
 
     slots = adj.shape[0]
 
@@ -252,12 +286,12 @@
         run[p] = total
         return total
 
-    lax.fori_loop(0, slots, forward, jnp.zeros((BLK, BLK), F32), unroll=8)
+    lax.fori_loop(0, slots, forward, jnp.zeros((BLK, BLK), F32), unroll=64)
 
     def row_block(b):
         return run[idx_ref[2, b]] * flt_ref[1, b]
 
-    order = [(pair_step, step) for step in (2, 1, -1, 0) for pair_step in (1, 0)]
+    order = [(pair_step, step) for pair_step in (1, 0) for step in (2, 1, -1, 0)]
 
     def spot(pair, pos, step):
         return pair * 4 + (pos + step) % 4
@@ -270,7 +304,7 @@
             rsend[q * SHARD + b] = row_block((q * 2 + 1 - core) * SHARD + b).astype(BF16)
             return 0
 
-        lax.fori_loop(0, SHARD, fill, 0)
+        lax.fori_loop(0, SHARD, fill, 0, unroll=SHARD)
         line = core_lines[pair_step, step] = lines.line()
         place = pl.ds(q * SHARD, SHARD)
         lines.send(line, rsend.at[place], crecv.at[place], other)
@@ -283,7 +317,7 @@
             rown[q * SHARD + b] = row_block((q * 2 + core) * SHARD + b) + crecv[q * SHARD + b].astype(F32)
             return 0
 
-        lax.fori_loop(0, SHARD, fill, 0)
+        lax.fori_loop(0, SHARD, fill, 0, unroll=SHARD)
 
     class Scatter:
         def __init__(self, s1, r1, s2, r2, xs, xr, term, ring, mate):
@@ -300,7 +334,7 @@
                     self.s1[pair_step * SHARD + b] = self.term(pair_step, 2, b).astype(BF16)
                     return 0
 
-                lax.fori_loop(0, HALF, fill, 0)
+                lax.fori_loop(0, HALF, fill, 0, unroll=HALF)
                 place = pl.ds(pair_step * SHARD + d * HALF, HALF)
                 lines.send(self.l1[pair_step][d], self.s1.at[place], self.r1.at[place], self.ring(1 - 2 * d))
 
@@ -318,7 +352,7 @@
                 self.s2[base + b] = value.astype(BF16)
                 return 0
 
-            lax.fori_loop(0, HALF, fill, 0)
+            lax.fori_loop(0, HALF, fill, 0, unroll=HALF)
             place = pl.ds(base, HALF)
             lines.send(self.l2[pair_step][d][h], self.s2.at[place], self.r2.at[place], self.ring(1 - 2 * d))
 
@@ -338,7 +372,7 @@
                 self.xs[h * HALF + b] = self.total(1, h * HALF + b).astype(BF16)
                 return 0
 
-            lax.fori_loop(0, HALF, fill, 0)
+            lax.fori_loop(0, HALF, fill, 0, unroll=HALF)
             place = pl.ds(h * HALF, HALF)
             lines.send(self.lx[h], self.xs.at[place], self.xr.at[place], self.mate)
 
@@ -351,7 +385,7 @@
                 use(b, self.total(0, b) + self.xr[b].astype(F32))
                 return 0
 
-            lax.fori_loop(0, HALF, body, 0)
+            lax.fori_loop(0, HALF, body, 0, unroll=HALF)
 
     def row_term(pair_step, step, b):
         return rown[spot(1 - xl if pair_step else xl, z, step) * SHARD + b]
@@ -360,12 +394,19 @@
     for pair_step in (1, 0):
         add_core(pair_step, 2)
         rows_s.far(pair_step)
-    for pair_step in (1, 0):
         for d in range(2):
             add_core(pair_step, 1 - 2 * d)
             rows_s.near(pair_step, d, False)
-    for pair_step in (1, 0):
         add_core(pair_step, 0)
+        if pair_step == 1:
+            for d in range(2):
+                cols_g.got_ring(1, d, 1 - d)
+                cross(1, 2 * d - 1, 1 - d)
+            for d in range(2):
+                cols_g.got_far(1, d)
+                cross(1, 2, d)
+            for d in range(2):
+                rows_s.near(1, d, True)
 
     for line, there in across:
         lines.wait(line, there, other)
@@ -375,27 +416,29 @@
         run[p] = total
         return total
 
-    lax.fori_loop(0, slots, backward, jnp.zeros((BLK, BLK), F32), unroll=8)
+    lax.fori_loop(0, slots, backward, jnp.zeros((BLK, BLK), F32), unroll=32)
+
+    collect(col_mates, bias_lines, bias_col)
+    bias_row[row] = added(bias_col)
+    bias_lines = spread(row_mates, lambda theirs: bias_row.at[row], bias_row, row)
 
     def col_term(pair_step, step, b):
         at = spot(1 - xh if pair_step else xh, y, step) * SHARD + b
         return run[idx_ref[5, at]] * flt_ref[3, at]
 
     cols_s = Scatter(ys1, yr1, ys2, yr2, yxs, yxr, col_term, at_y, pair_x)
-    for pair_step in (1, 0):
-        cols_s.far(pair_step)
-    for pair_step in (1, 0):
-        for d in range(2):
-            cols_s.near(pair_step, d, False)
-    for pair_step in (1, 0):
-        for d in range(2):
-            rows_s.near(pair_step, d, True)
+    cols_s.far(1)
+    for d in range(2):
+        cols_s.near(1, d, False)
     for h in range(2):
         rows_s.swap(h)
-    for pair_step in (1, 0):
-        for d in range(2):
-            cols_s.near(pair_step, d, True)
-
+    for d in range(2):
+        rows_s.near(0, d, True)
+    for d in range(2):
+        cols_s.near(1, d, True)
+    cols_s.far(0)
+    for d in range(2):
+        cols_s.near(0, d, False)
     def layer(b, value):
         nodes = pl.ds(pl.multiple_of(b * BLK, BLK), BLK)
         sums = value.astype(BF16)
@@ -410,50 +453,23 @@
         nodes = pl.ds(pl.multiple_of(b * BLK, BLK), BLK)
         return total + lax.dot_general(agg[b], gpre[nodes, :], (((0,), (0,)), ((), ())), preferred_element_type=F32)
 
-    gw_ref[...] = lax.fori_loop(0, SHARD, weight_term, jnp.zeros(gw_ref.shape, F32))
-
-    pieces = gsum.shape[0]
-    depth = gw_ref.shape[0] // pieces
+    gw_ref[...] = lax.fori_loop(0, SHARD, weight_term, jnp.zeros(gw_ref.shape, F32), unroll=SHARD)
+
+    pieces, depth = gsum.shape[0], gsum.shape[1]
     for n in range(pieces):
-        gsum[n, pl.ds(0, depth), :] = gw_ref[pl.ds(n * depth, depth), :]
-        gsum[n, pl.ds(depth, 8), :] = jnp.broadcast_to(gb_ref[...], (8, gb_ref.shape[1]))
-    line = lines.line()
-    lines.send(line, gsum.at[pl.ds((1 - core) * 4, 4)], ar_core, other)
+        gsum[n] = gw_ref[pl.ds(n * depth, depth), :]
+    used = spread(col_mates, lambda theirs: gsum.at[theirs], ar_col, col)
+    ar_col[col] = gsum[col]
     for h in range(2):
         cols_s.swap(h)
-    lines.wait(line, ar_core, other)
-    for n in range(4):
-        ar_core[n] = ar_core[n] + gsum[core * 4 + n]
-
-    z_lines = [lines.line() for _ in range(3)]
-    for step in (2, 1, 3):
-        lines.send(z_lines[step - 1], ar_core.at[(z + step) % 4], ar_z.at[step], at_z(step))
-    ar_z[0] = ar_core[z]
-    for step in (1, 2, 3):
-        lines.wait(z_lines[step - 1], ar_z.at[step], at_z(4 - step))
-    ar_y[y] = (ar_z[0] + ar_z[1]) + (ar_z[2] + ar_z[3])
-    y_lines = [lines.line() for _ in range(3)]
-    for step in (2, 1, 3):
-        lines.send(y_lines[step - 1], ar_y.at[y], ar_y.at[y], at_y(step))
-    for step in (1, 2, 3):
-        lines.wait(y_lines[step - 1], ar_y.at[(y + 4 - step) % 4], at_y(4 - step))
-    x = xh * 2 + xl
-    ar_x[x] = (ar_y[0] + ar_y[1]) + (ar_y[2] + ar_y[3])
-    x_mates = [(near_x, xh * 2 + 1 - xl), (pair_x, (1 - xh) * 2 + xl), (diag_x, (1 - xh) * 2 + 1 - xl)]
-    x_lines = [lines.line() for _ in range(3)]
-    for line, (mate, _) in zip(x_lines, x_mates):
-        lines.send(line, ar_x.at[x], ar_x.at[x], mate)
-    for line, (mate, place) in zip(x_lines, x_mates):
-        lines.wait(line, ar_x.at[place], mate)
-    mine = core * 4 + z
-    gall[mine] = (ar_x[0] + ar_x[1]) + (ar_x[2] + ar_x[3])
-    e_lines = [lines.line() for _ in range(3)]
-    for step in (2, 1, 3):
-        lines.send(e_lines[step - 1], gall.at[mine], gall.at[mine], at_z(step))
-    for step in (1, 2, 3):
-        lines.wait(e_lines[step - 1], gall.at[core * 4 + (z + 4 - step) % 4], at_z(4 - step))
-    line = lines.line()
-    lines.send(line, gall.at[pl.ds(core * 4, 4)], gall.at[pl.ds(core * 4, 4)], other)
+    for d in range(2):
+        cols_s.near(0, d, True)
+    collect(col_mates, used, ar_col)
+    ar_row[row] = added(ar_col)
+    used = spread(row_mates, lambda theirs: ar_row.at[row], ar_row, row)
+    collect(row_mates, used, ar_row)
+    gall[col] = added(ar_row)
+    used = spread(col_mates, lambda theirs: gall.at[col], gall, col)
 
     def store(b, value):
         gf_ref[b] = jnp.transpose(value).astype(BF16)
@@ -461,10 +477,11 @@
     for h in range(2):
         cols_s.finish(h, store)
 
-    lines.wait(line, gall.at[pl.ds((1 - core) * 4, 4)], other)
+    collect(row_mates, bias_lines, bias_row)
+    gb_ref[...] = added(bias_row)[:1]
+    collect(col_mates, used, gall)
     for n in range(pieces):
-        gw_ref[pl.ds(n * depth, depth), :] = gall[n, pl.ds(0, depth), :]
-    gb_ref[...] = gall[0, pl.ds(depth, 1), :]
+        gw_ref[pl.ds(n * depth, depth), :] = gall[n]
     lines.drain()
     assert lines.used <= N_LINES
 
@@ -485,14 +502,15 @@
         return pltpu.VMEM((n, BLK, BLK), dtype)
 
     scratch = [
+        pltpu.VMEM((1024, hid), BF16), pltpu.VMEM((1024, hid), jnp.int32),
         blocks(slots), blocks(slots, F32), blocks(64), blocks(128), pltpu.VMEM((1024, hid), BF16),
         blocks(64), blocks(64), blocks(64, F32)]
     for _ in range(2):
         scratch += [blocks(16), blocks(16), blocks(32), blocks(32), blocks(8), blocks(8)]
-    piece = (24, hid)
-    scratch += [blocks(8), pltpu.VMEM((8,) + piece, F32)]
-    scratch += [pltpu.VMEM((4,) + piece, F32) for _ in range(4)] + [pltpu.VMEM((8,) + piece, F32)]
-    scratch += [pltpu.SemaphoreType.DMA((N_LINES,)), pltpu.SemaphoreType.DMA((N_LINES,)), pltpu.SemaphoreType.DMA]
+    piece = (8, hid)
+    scratch += [blocks(8)] + [pltpu.VMEM((n,) + piece, F32) for n in (16, 16, 8, 16)]
+    scratch += [pltpu.VMEM(piece, F32)] + [pltpu.VMEM((n,) + piece, F32) for n in (16, 8)]
+    scratch += [pltpu.SemaphoreType.DMA((N_LINES,)), pltpu.SemaphoreType.DMA((N_LINES,)), pltpu.SemaphoreType.DMA((3,))]
     out, gf, gw, gb = pl.pallas_call(
         layer_kernel,
         out_shape=(
@@ -501,13 +519,21 @@
             jax.ShapeDtypeStruct(weight.shape, F32),
             jax.ShapeDtypeStruct((1, hid), F32),
         ),
-        in_specs=[smem, smem, vmem, vmem, vmem, vmem, vmem, hbm],
+        in_specs=[smem, smem, vmem, vmem, vmem, hbm, hbm, hbm],
         out_specs=(vmem, vmem, vmem, vmem),
         scratch_shapes=scratch,
         compiler_params=pltpu.CompilerParams(collective_id=0, has_side_effects=True, vmem_limit_bytes=60 * 2**20),
         name="layer",
     )(idx, flt, features.reshape(SHARD, BLK, BLK), weight, bias.reshape(1, hid), cotangent, relu_mask,
       adjacency.reshape(slots, BLK, BLK))
+    results = (out, gf, gw, gb)
+    out, gf, gw, gb = pl.pallas_call(
+        hand_on_kernel,
+        out_shape=tuple(jax.ShapeDtypeStruct(r.shape, r.dtype) for r in results),
+        in_specs=[vmem] * 4,
+        out_specs=(vmem,) * 4,
+        name="hand_on",
+    )(*results)
     return out, gf.reshape(1024, BLK), gw, gb.reshape(hid)
 
 

time: 97.1 us -> 77.2 us (0.80)
  Pallas kernels: 89.2 us -> 75.8 us
  local copies, waits for them, and re-layouts: 6.33 us -> 0 us
    pallas_call x1, Pallas kernels: 87.4 us -> 71.9 us  [local(): pl.pallas_call(layer_kernel, out_shape=(jax.ShapeDtypeStruct((1024, hid),...]
    unnamed x4 -> x0, local copies, waits for them, and re-layouts: 6.33 us -> none
    pallas_call x0 -> x1, Pallas kernels: none -> 2.08 us  [local(): pl.pallas_call(hand_on_kernel, out_shape=tuple((jax.ShapeDtypeStruct(r.sh...]
where the time goes in v2:
time: 77.2 us; the launch traced here: 77.1 us
  Pallas kernels  75.8 us (98%)
  between operations  1.29 us (2%)
    pallas_call x1, Pallas kernels, local(): pl.pallas_call(layer_kernel, out_shape=(jax.ShapeDtypeStruct((1024, hid),...  71.9 us
    pallas_call x1, Pallas kernels, local(): pl.pallas_call(hand_on_kernel, out_shape=tuple((jax.ShapeDtypeStruct(r.sh...  2.08 us
    pallas_call x1, Pallas kernels, local(): pl.pallas_call(plan_kernel, out_shape=(jax.ShapeDtypeStruct((8, slots), j...  1.82 us

profile of v2, /device:TPU:1, one launch (start us, length us, event | category | flops | bytes accessed | tf_op | source)
XLA Modules:
  0.0 77.1 jit_solution(7648554131993583499)
XLA Ops:
  1.3 1.8 %plan.1 = (s32[8,256]{1,0:T(8,128)}, f32[8,256]{1,0:T(8,128)}) custom-call(s32[1,1]{1,0:T(1,128)S(6)} %copy.13.count_ref, s32[1,256]{1,0:T(1,128)} %bitcast.9, s32[1,256]{1,0:T(1,128)} %bitcast.10), custom_call_target="tpu_custom_call" | custom-call | tf_op jit(solution)/shard_map/plan/pallas_call | solution.py:492
  3.1 71.9 %layer.1 = (bf16[1024,256]{1,0:T(8,128)(2,1)}, bf16[8,128,128]{2,1,0:T(8,128)(2,1)}, f32[128,256]{1,0:T(8,128)}, f32[1,256]{1,0:T(1,128)}) custom-call(s32[8,256]{1,0:T(8,128)} %get-tuple-element.14.idx_ref, f32[8,256]{1,0:T(8,128)} %get-tuple-element.15.flt_ref, bf16[8,128,128]{2,1,0:T(8,128)(2,1)} %bitcast.8, bf16[128,256]{1,0:T(8,128)(2,1)} %weight_ref.1, ...), custom_call_target="tpu_custom_call" | custom-call | tf_op jit(solution)/shard_map/layer/pallas_call | solution.py:514
  75.0 2.1 %hand_on.1 = (bf16[1024,256]{1,0:T(8,128)(2,1)}, bf16[8,128,128]{2,1,0:T(8,128)(2,1)}, f32[128,256]{1,0:T(8,128)}, f32[1,256]{1,0:T(1,128)}) custom-call(bf16[1024,256]{1,0:T(8,128)(2,1)} %get-tuple-element.16.refs_0_, bf16[8,128,128]{2,1,0:T(8,128)(2,1)} %get-tuple-element.17.refs_1_, f32[128,256]{1,0:T(8,128)} %get-tuple-element.18.refs_2_, ...), custom_call_target="tpu_custom_call" | custom-call | tf_op jit(solution)/shard_map/hand_on/pallas_call | solution.py:530

commit v3 on v2

--- a/solution.py
+++ b/solution.py
@@ -15,41 +15,39 @@
 HALF = 4
 
 
-def plan_kernel(count_ref, rows_ref, cols_ref, idx_ref, flt_ref):
+def plan(count_ref, rows_ref, cols_ref, idx_ref, flt_ref):
     n = rows_ref.shape[1]
     count = count_ref[0, 0]
     lane = lax.broadcasted_iota(jnp.int32, (n, n), 1)
     sub = lax.broadcasted_iota(jnp.int32, (n, n), 0)
-    lane_f, sub_f = lane.astype(F32), sub.astype(F32)
+    one, zero = jnp.ones((n, n), jnp.int32), jnp.zeros((n, n), jnp.int32)
     eye = lane == sub
     live_l, live_c = lane < count, sub < count
-    row_l = jnp.broadcast_to(rows_ref[...].astype(F32), (n, n))
-    col_l = jnp.broadcast_to(cols_ref[...].astype(F32), (n, n))
-    zero = jnp.zeros((n, n), F32)
+    row_l = jnp.broadcast_to(rows_ref[...], (n, n))
+    col_l = jnp.broadcast_to(cols_ref[...], (n, n))
     row_c = jnp.broadcast_to(jnp.sum(jnp.where(eye, row_l, zero), axis=1, keepdims=True), (n, n))
     col_c = jnp.broadcast_to(jnp.sum(jnp.where(eye, col_l, zero), axis=1, keepdims=True), (n, n))
     idx_ref[...] = jnp.zeros_like(idx_ref)
     flt_ref[...] = jnp.zeros_like(flt_ref)
-    one = jnp.ones((n, n), F32)
+    tops = (127, 63)
     for side, (major_l, major_c, minor_c) in enumerate(((row_l, row_c, col_c), (col_l, col_c, row_c))):
-        far = jnp.full((n, n), 65536.0, F32)
-        key_l = jnp.where(live_l, major_l * n, far) + lane_f
-        key_c = jnp.where(live_c, major_c * n, far) + sub_f
+        far = jnp.full((n, n), 65536, jnp.int32)
+        key_l = jnp.where(live_l, major_l * n, far) + lane
+        key_c = jnp.where(live_c, major_c * n, far) + sub
         rank = jnp.sum(jnp.where(key_l < key_c, one, zero), axis=1, keepdims=True)
-        hot = jnp.where(jnp.broadcast_to(rank, (n, n)) == lane_f, one, zero)
-        same = jnp.where(major_l == major_c, one, zero) * jnp.where(lane < sub, one, zero) * jnp.where(live_l, one, zero)
-        keep = jnp.where(jnp.sum(same, axis=1, keepdims=True) > 0.5, 1.0, 0.0)
-        slot = jnp.sum(hot * sub_f, axis=0, keepdims=True)
-        minor = jnp.sum(hot * minor_c, axis=0, keepdims=True)
-        keep_sorted = jnp.sum(hot * keep, axis=0, keepdims=True)
-        live_f = jnp.where(live_c, one, zero)
-        upto = jnp.sum(jnp.where(major_c <= lane_f, live_f, zero), axis=0, keepdims=True)
-        here = jnp.sum(jnp.where(major_c == lane_f, live_f, zero), axis=0, keepdims=True)
-        idx_ref[3 * side : 3 * side + 1, :] = slot.astype(jnp.int32)
-        idx_ref[3 * side + 1 : 3 * side + 2, :] = minor.astype(jnp.int32)
-        idx_ref[3 * side + 2 : 3 * side + 3, :] = jnp.maximum(upto - 1.0, 0.0).astype(jnp.int32)
-        flt_ref[2 * side : 2 * side + 1, :] = keep_sorted
-        flt_ref[2 * side + 1 : 2 * side + 2, :] = jnp.where(here > 0.5, 1.0, 0.0)
+        hot = jnp.broadcast_to(rank, (n, n)) == lane
+        same = jnp.where((major_l == major_c) & (lane < sub) & live_l, one, zero)
+        keep = jnp.broadcast_to(jnp.minimum(jnp.sum(same, axis=1, keepdims=True), 1), (n, n))
+        slot = jnp.sum(jnp.where(hot, sub, zero), axis=0, keepdims=True)
+        minor = jnp.sum(jnp.where(hot, minor_c, zero), axis=0, keepdims=True)
+        keep_sorted = jnp.sum(jnp.where(hot, keep, zero), axis=0, keepdims=True)
+        upto = jnp.sum(jnp.where((major_c <= lane) & live_c, one, zero), axis=0, keepdims=True)
+        here = jnp.sum(jnp.where((major_c == lane) & live_c, one, zero), axis=0, keepdims=True)
+        idx_ref[3 * side : 3 * side + 1, :] = jnp.clip(slot, 0, n - 1)
+        idx_ref[3 * side + 1 : 3 * side + 2, :] = jnp.clip(minor, 0, tops[1 - side])
+        idx_ref[3 * side + 2 : 3 * side + 3, :] = jnp.clip(upto - 1, 0, n - 1)
+        flt_ref[2 * side : 2 * side + 1, :] = keep_sorted.astype(F32)
+        flt_ref[2 * side + 1 : 2 * side + 2, :] = jnp.minimum(here, 1).astype(F32)
 
 
 def hand_on_kernel(*refs):
@@ -87,9 +85,9 @@
 
 
 def layer_kernel(
-    idx_ref, flt_ref, feat_ref, weight_ref, bias_ref, cot_hbm, mask_hbm, adj_ref,
+    count_ref, rows_ref, cols_ref, feat_ref, weight_ref, bias_ref, cot_hbm, mask_hbm, adj_ref,
     out_ref, gf_ref, gw_ref, gb_ref,
-    cot_ref, mask_ref, adj, run, feats, proj, gpre, rsend, crecv, rown,
+    idx_vmem, flt_vmem, idx_ref, flt_ref, cot_ref, mask_ref, adj, run, feats, proj, gpre, rsend, crecv, rown,
     zs1, zr1, zs2, zr2, zxs, zxr, ys1, yr1, ys2, yr2, yxs, yxr,
     agg, gsum, ar_col, ar_row, gall, bias_own, bias_col, bias_row,
     send_sems, recv_sems, in_sems):
@@ -222,6 +220,11 @@
 
     cross(0, 0, 0)
     cross(0, 0, 1)
+    plan(count_ref, rows_ref, cols_ref, idx_vmem, flt_vmem)
+    idx_copy = pltpu.make_async_copy(idx_vmem, idx_ref, in_sems.at[3])
+    flt_copy = pltpu.make_async_copy(flt_vmem, flt_ref, in_sems.at[4])
+    idx_copy.start()
+    flt_copy.start()
     for d in range(2):
         rows_g.got_ring(0, d, d)
         rows_g.pass_ring(0, d)
@@ -258,6 +261,8 @@
     for d in range(2):
         rows_g.got_far(1, d)
     adj_copy.wait()
+    idx_copy.wait()
+    flt_copy.wait()
 
     def spread(mates, source, target, place):
         used = [lines.line() for _ in mates]
@@ -275,9 +280,9 @@
             total = total + ref[n]
         return total
 
-    bias_own[...] = jnp.broadcast_to(gb_ref[...], bias_own.shape)
-    bias_col[col] = bias_own[...]
-    bias_lines = spread(col_mates, lambda theirs: bias_own, bias_col, col)
+    bias_own[0] = gb_ref[...]
+    bias_col[col] = gb_ref[...]
+    bias_lines = spread(col_mates, lambda theirs: bias_own.at[0], bias_col, col)
 
     slots = adj.shape[0]
 
@@ -291,7 +296,7 @@
     def row_block(b):
         return run[idx_ref[2, b]] * flt_ref[1, b]
 
-    order = [(pair_step, step) for pair_step in (1, 0) for step in (2, 1, -1, 0)]
+    order = [(1, 2), (1, 1), (1, -1), (0, 1), (0, -1), (0, 2), (1, 0), (0, 0)]
 
     def spot(pair, pos, step):
         return pair * 4 + (pos + step) % 4
@@ -320,34 +325,42 @@
         lax.fori_loop(0, SHARD, fill, 0, unroll=SHARD)
 
     class Scatter:
-        def __init__(self, s1, r1, s2, r2, xs, xr, term, ring, mate):
+        def __init__(self, s1, r1, s2, r2, xs, xr, term, ring, mate, far_by_mate):
             self.s1, self.r1, self.s2, self.r2, self.xs, self.xr = s1, r1, s2, r2, xs, xr
-            self.term, self.ring, self.mate = term, ring, mate
+            self.term, self.ring, self.mate, self.far_by_mate = term, ring, mate, far_by_mate
             self.l1 = [[lines.line() for _ in range(2)] for _ in range(2)]
             self.l2 = [[[lines.line() for _ in range(2)] for _ in range(2)] for _ in range(2)]
             self.lx = [lines.line() for _ in range(2)]
 
         def far(self, pair_step):
             for d in range(2):
+                if self.far_by_mate and pair_step == 0:
+                    lines.wait(self.l1[1][d], self.r1.at[pl.ds(SHARD + d * HALF, HALF)], self.mate)
+
                 def fill(b, _, d=d):
                     b = d * HALF + b
-                    self.s1[pair_step * SHARD + b] = self.term(pair_step, 2, b).astype(BF16)
+                    value = self.term(pair_step, 2, b)
+                    if self.far_by_mate and pair_step == 0:
+                        value = value + self.r1[SHARD + b].astype(F32)
+                    self.s1[pair_step * SHARD + b] = value.astype(BF16)
                     return 0
 
                 lax.fori_loop(0, HALF, fill, 0, unroll=HALF)
                 place = pl.ds(pair_step * SHARD + d * HALF, HALF)
-                lines.send(self.l1[pair_step][d], self.s1.at[place], self.r1.at[place], self.ring(1 - 2 * d))
+                lines.send(self.l1[pair_step][d], self.s1.at[place], self.r1.at[place],
+                           self.mate if self.far_by_mate and pair_step else self.ring(1 - 2 * d))
 
         def near(self, pair_step, d, late):
             h = d if late else 1 - d
             base = (pair_step * 2 + d) * SHARD + h * HALF
-            if late:
+            passing = late and not (self.far_by_mate and pair_step)
+            if passing:
                 place = pl.ds(pair_step * SHARD + d * HALF, HALF)
                 lines.wait(self.l1[pair_step][d], self.r1.at[place], self.ring(2 * d - 1))
 
             def fill(b, _):
                 value = self.term(pair_step, 1 - 2 * d, h * HALF + b)
-                if late:
+                if passing:
                     value = value + self.r1[pair_step * SHARD + d * HALF + b].astype(F32)
                 self.s2[base + b] = value.astype(BF16)
                 return 0
@@ -390,23 +403,26 @@
     def row_term(pair_step, step, b):
         return rown[spot(1 - xl if pair_step else xl, z, step) * SHARD + b]
 
-    rows_s = Scatter(zs1, zr1, zs2, zr2, zxs, zxr, row_term, at_z, near_x)
+    rows_s = Scatter(zs1, zr1, zs2, zr2, zxs, zxr, row_term, at_z, near_x, True)
+    add_core(1, 2)
+    rows_s.far(1)
+    for d in range(2):
+        add_core(1, 1 - 2 * d)
+        rows_s.near(1, d, False)
+    for d in range(2):
+        rows_s.near(1, d, True)
+    for d in range(2):
+        add_core(0, 1 - 2 * d)
+        rows_s.near(0, d, False)
+    add_core(0, 2)
     for pair_step in (1, 0):
-        add_core(pair_step, 2)
-        rows_s.far(pair_step)
-        for d in range(2):
-            add_core(pair_step, 1 - 2 * d)
-            rows_s.near(pair_step, d, False)
         add_core(pair_step, 0)
-        if pair_step == 1:
-            for d in range(2):
-                cols_g.got_ring(1, d, 1 - d)
-                cross(1, 2 * d - 1, 1 - d)
-            for d in range(2):
-                cols_g.got_far(1, d)
-                cross(1, 2, d)
-            for d in range(2):
-                rows_s.near(1, d, True)
+    for d in range(2):
+        cols_g.got_ring(1, d, 1 - d)
+        cross(1, 2 * d - 1, 1 - d)
+    for d in range(2):
+        cols_g.got_far(1, d)
+        cross(1, 2, d)
 
     for line, there in across:
         lines.wait(line, there, other)
@@ -418,36 +434,40 @@
 
     lax.fori_loop(0, slots, backward, jnp.zeros((BLK, BLK), F32), unroll=32)
 
+    def col_term(pair_step, step, b):
+        at = spot(1 - xh if pair_step else xh, y, step) * SHARD + b
+        return run[idx_ref[5, at]] * flt_ref[3, at]
+
+    cols_s = Scatter(ys1, yr1, ys2, yr2, yxs, yxr, col_term, at_y, pair_x, False)
+    cols_s.far(1)
+    for d in range(2):
+        cols_s.near(1, d, False)
+    rows_s.far(0)
+    for h in range(2):
+        rows_s.swap(h)
+    for d in range(2):
+        cols_s.near(1, d, True)
+    cols_s.far(0)
+    for d in range(2):
+        cols_s.near(0, d, False)
+    for d in range(2):
+        rows_s.near(0, d, True)
+
     collect(col_mates, bias_lines, bias_col)
     bias_row[row] = added(bias_col)
     bias_lines = spread(row_mates, lambda theirs: bias_row.at[row], bias_row, row)
 
-    def col_term(pair_step, step, b):
-        at = spot(1 - xh if pair_step else xh, y, step) * SHARD + b
-        return run[idx_ref[5, at]] * flt_ref[3, at]
-
-    cols_s = Scatter(ys1, yr1, ys2, yr2, yxs, yxr, col_term, at_y, pair_x)
-    cols_s.far(1)
-    for d in range(2):
-        cols_s.near(1, d, False)
+    def aggregate(b, value):
+        agg[b] = value.astype(BF16)
+
+    def layer(b, _):
+        nodes = pl.ds(pl.multiple_of(b * BLK, BLK), BLK)
+        pre = jnp.dot(agg[b], weight_ref[...], preferred_element_type=F32) + bias_ref[...]
+        out_ref[nodes, :] = (pre * mask_ref[nodes, :].astype(F32)).astype(BF16)
+        return 0
+
     for h in range(2):
-        rows_s.swap(h)
-    for d in range(2):
-        rows_s.near(0, d, True)
-    for d in range(2):
-        cols_s.near(1, d, True)
-    cols_s.far(0)
-    for d in range(2):
-        cols_s.near(0, d, False)
-    def layer(b, value):
-        nodes = pl.ds(pl.multiple_of(b * BLK, BLK), BLK)
-        sums = value.astype(BF16)
-        agg[b] = sums
-        pre = jnp.dot(sums, weight_ref[...], preferred_element_type=F32) + bias_ref[...]
-        out_ref[nodes, :] = (pre * mask_ref[nodes, :].astype(F32)).astype(BF16)
-
-    for h in range(2):
-        rows_s.finish(h, layer)
+        rows_s.finish(h, aggregate)
 
     def weight_term(b, total):
         nodes = pl.ds(pl.multiple_of(b * BLK, BLK), BLK)
@@ -460,6 +480,7 @@
         gsum[n] = gw_ref[pl.ds(n * depth, depth), :]
     used = spread(col_mates, lambda theirs: gsum.at[theirs], ar_col, col)
     ar_col[col] = gsum[col]
+    lax.fori_loop(0, SHARD, layer, 0, unroll=SHARD)
     for h in range(2):
         cols_s.swap(h)
     for d in range(2):
@@ -478,7 +499,7 @@
         cols_s.finish(h, store)
 
     collect(row_mates, bias_lines, bias_row)
-    gb_ref[...] = added(bias_row)[:1]
+    gb_ref[...] = added(bias_row)
     collect(col_mates, used, gall)
     for n in range(pieces):
         gw_ref[pl.ds(n * depth, depth), :] = gall[n]
@@ -489,19 +510,14 @@
 def local(features, weight, bias, adjacency, block_rows, block_cols, block_count, cotangent, relu_mask):
     slots = adjacency.shape[2]
     vmem, smem, hbm = (pl.BlockSpec(memory_space=m) for m in (pltpu.VMEM, pltpu.SMEM, pl.ANY))
-    idx, flt = pl.pallas_call(
-        plan_kernel,
-        out_shape=(jax.ShapeDtypeStruct((8, slots), jnp.int32), jax.ShapeDtypeStruct((8, slots), F32)),
-        in_specs=[smem, vmem, vmem],
-        out_specs=(vmem, vmem),
-        name="plan",
-    )(block_count, block_rows[0], block_cols[0])
     hid = weight.shape[1]
 
     def blocks(n, dtype=BF16):
         return pltpu.VMEM((n, BLK, BLK), dtype)
 
+    plan_shape = (8, slots)
     scratch = [
+        pltpu.VMEM(plan_shape, jnp.int32), pltpu.VMEM(plan_shape, F32), pltpu.SMEM(plan_shape, jnp.int32), pltpu.SMEM(plan_shape, F32),
         pltpu.VMEM((1024, hid), BF16), pltpu.VMEM((1024, hid), jnp.int32),
         blocks(slots), blocks(slots, F32), blocks(64), blocks(128), pltpu.VMEM((1024, hid), BF16),
         blocks(64), blocks(64), blocks(64, F32)]
@@ -509,8 +525,8 @@
         scratch += [blocks(16), blocks(16), blocks(32), blocks(32), blocks(8), blocks(8)]
     piece = (8, hid)
     scratch += [blocks(8)] + [pltpu.VMEM((n,) + piece, F32) for n in (16, 16, 8, 16)]
-    scratch += [pltpu.VMEM(piece, F32)] + [pltpu.VMEM((n,) + piece, F32) for n in (16, 8)]
-    scratch += [pltpu.SemaphoreType.DMA((N_LINES,)), pltpu.SemaphoreType.DMA((N_LINES,)), pltpu.SemaphoreType.DMA((3,))]
+    scratch += [pltpu.VMEM((n, 1, hid), F32) for n in (1, 16, 8)]
+    scratch += [pltpu.SemaphoreType.DMA((N_LINES,)), pltpu.SemaphoreType.DMA((N_LINES,)), pltpu.SemaphoreType.DMA((5,))]
     out, gf, gw, gb = pl.pallas_call(
         layer_kernel,
         out_shape=(
@@ -519,12 +535,12 @@
             jax.ShapeDtypeStruct(weight.shape, F32),
             jax.ShapeDtypeStruct((1, hid), F32),
         ),
-        in_specs=[smem, smem, vmem, vmem, vmem, hbm, hbm, hbm],
+        in_specs=[smem, vmem, vmem, vmem, vmem, vmem, hbm, hbm, hbm],
         out_specs=(vmem, vmem, vmem, vmem),
         scratch_shapes=scratch,
         compiler_params=pltpu.CompilerParams(collective_id=0, has_side_effects=True, vmem_limit_bytes=60 * 2**20),
         name="layer",
-    )(idx, flt, features.reshape(SHARD, BLK, BLK), weight, bias.reshape(1, hid), cotangent, relu_mask,
+    )(block_count, block_rows[0], block_cols[0], features.reshape(SHARD, BLK, BLK), weight, bias.reshape(1, hid), cotangent, relu_mask,
       adjacency.reshape(slots, BLK, BLK))
     results = (out, gf, gw, gb)
     out, gf, gw, gb = pl.pallas_call(

time: 77.2 us -> 74.8 us (0.969)
  Pallas kernels: 75.8 us -> 73.3 us
    pallas_call x1 -> x0, Pallas kernels: 1.82 us -> none  [local(): pl.pallas_call(plan_kernel, out_shape=(jax.ShapeDtypeStruct((8, slots), j...]
where the time goes in v3:
time: 74.8 us; the launch traced here: 74.6 us
  Pallas kernels  73.3 us (98%)
  between operations  1.29 us (2%)
    pallas_call x1, Pallas kernels, local(): pl.pallas_call(layer_kernel, out_shape=(jax.ShapeDtypeStruct((1024, hid),...  71.2 us
    pallas_call x1, Pallas kernels, local(): pl.pallas_call(hand_on_kernel, out_shape=tuple((jax.ShapeDtypeStruct(r.sh...  2.08 us

profile of v3, /device:TPU:1, one launch (start us, length us, event | category | flops | bytes accessed | tf_op | source)
XLA Modules:
  0.0 74.6 jit_solution(7201761710677481408)
XLA Ops:
  1.3 71.2 %layer.1 = (bf16[1024,256]{1,0:T(8,128)(2,1)}, bf16[8,128,128]{2,1,0:T(8,128)(2,1)}, f32[128,256]{1,0:T(8,128)}, f32[1,256]{1,0:T(1,128)}) custom-call(s32[1,1]{1,0:T(1,128)S(6)} %copy.13.count_ref, s32[1,256]{1,0:T(1,128)} %bitcast.9, s32[1,256]{1,0:T(1,128)} %bitcast.10, bf16[8,128,128]{2,1,0:T(8,128)(2,1)} %bitcast.8, bf16[128,256]{1,0:T(8,128)(2,1)} %weight_ref.1, ...), custom_call_target="tpu_custom_call" | custom-call | tf_op jit(solution)/shard_map/layer/pallas_call | solution.py:530
  72.5 2.1 %hand_on.1 = (bf16[1024,256]{1,0:T(8,128)(2,1)}, bf16[8,128,128]{2,1,0:T(8,128)(2,1)}, f32[128,256]{1,0:T(8,128)}, f32[1,256]{1,0:T(1,128)}) custom-call(bf16[1024,256]{1,0:T(8,128)(2,1)} %get-tuple-element.12.refs_0_, bf16[8,128,128]{2,1,0:T(8,128)(2,1)} %get-tuple-element.13.refs_1_, f32[128,256]{1,0:T(8,128)} %get-tuple-element.14.refs_2_, ...), custom_call_target="tpu_custom_call" | custom-call | tf_op jit(solution)/shard_map/hand_on/pallas_call | solution.py:546

commit v4 on v3

--- a/solution.py
+++ b/solution.py
@@ -157,6 +157,7 @@
             self.l2 = [lines.line() for _ in range(2)]
             self.l3 = [[lines.line() for _ in range(2)] for _ in range(2)]
             self.l4 = [lines.line() for _ in range(2)]
+            self.lf = lines.line()
 
         def place(self, pair_step, step, half):
             pair = self.pair if pair_step == 0 else 1 - self.pair
@@ -173,9 +174,8 @@
             lines.wait(self.l0[h], self.place(1, 0, h), self.mate)
             return self.place(1, 0, h)
 
-        def pass_mate(self, late, cross=True):
+        def pass_mate(self, h):
             for d in range(2):
-                h = (1 - d if late else d) if cross else late
                 lines.send(self.l3[d][h], self.place(1, 0, h), self.place(1, 0, h), self.ring(1 - 2 * d))
 
         def got_ring(self, kind, d, h):
@@ -190,6 +190,24 @@
             table = self.l2 if kind == 0 else self.l4
             place = self.place(kind, step, d)
             lines.send(table[d], place, place, self.ring(-step))
+
+        def quarter(self, step, d):
+            shard = self.shard(1 - self.pair, (self.pos + step) % 4)
+            return self.buf.at[pl.ds(shard * SHARD + d * (HALF // 2), HALF // 2)]
+
+        def pass_quarter(self, d):
+            place = self.quarter(2 * d - 1, d)
+            lines.send(self.l4[d], place, place, self.ring(1 - 2 * d))
+
+        def got_quarter(self, d):
+            lines.wait(self.l4[d], self.quarter(2, d), self.ring(2 * d - 1))
+
+        def far_to_mate(self):
+            place = self.place(0, 2, 1)
+            lines.send(self.lf, place, place, self.mate)
+
+        def far_from_mate(self):
+            lines.wait(self.lf, self.place(1, 2, 1), self.mate)
 
         def got_far(self, kind, d):
             step = 2 * d - 1
@@ -233,11 +251,15 @@
         cols_g.pass_ring(0, d)
     for h in range(2):
         rows_g.got_mate(h)
-    for late in range(2):
-        rows_g.pass_mate(late)
+    for h in range(2):
+        rows_g.pass_mate(h)
+    for d in (1, 0):
+        rows_g.got_far(0, d)
+        if d == 1:
+            rows_g.far_to_mate()
     for h in range(2):
         cols_g.got_mate(h)
-        cols_g.pass_mate(h, False)
+        cols_g.pass_mate(h)
     for d in range(2):
         cross(0, 2 * d - 1, d)
         cross(1, 0, d)
@@ -245,8 +267,8 @@
         cols_g.got_ring(0, d, 1 - d)
         cross(0, 2 * d - 1, 1 - d)
     for d in range(2):
-        rows_g.got_ring(1, d, d)
-        rows_g.pass_ring(1, d)
+        rows_g.got_ring(1, d, 0)
+        rows_g.pass_quarter(d)
     for d in range(2):
         cols_g.got_far(0, d)
         cross(0, 2, d)
@@ -256,10 +278,10 @@
         cross(1, 2 * d - 1, d)
     for d in range(2):
         rows_g.got_ring(0, d, 1 - d)
-        rows_g.got_far(0, d)
-        rows_g.got_ring(1, d, 1 - d)
-    for d in range(2):
-        rows_g.got_far(1, d)
+        rows_g.got_ring(1, d, 1)
+    for d in range(2):
+        rows_g.got_quarter(d)
+    rows_g.far_from_mate()
     adj_copy.wait()
     idx_copy.wait()
     flt_copy.wait()
@@ -538,7 +560,7 @@
         in_specs=[smem, vmem, vmem, vmem, vmem, vmem, hbm, hbm, hbm],
         out_specs=(vmem, vmem, vmem, vmem),
         scratch_shapes=scratch,
-        compiler_params=pltpu.CompilerParams(collective_id=0, has_side_effects=True, vmem_limit_bytes=60 * 2**20),
+        compiler_params=pltpu.CompilerParams(collective_id=0, has_side_effects=True, vmem_limit_bytes=51 * 2**20),
         name="layer",
     )(block_count, block_rows[0], block_cols[0], features.reshape(SHARD, BLK, BLK), weight, bias.reshape(1, hid), cotangent, relu_mask,
       adjacency.reshape(slots, BLK, BLK))

time: 74.8 us -> 80.6 us (1.078)
  local copies, waits for them, and re-layouts: 0 us -> 8.81 us
  Pallas kernels: 73.3 us -> 70.1 us
    unnamed x0 -> x22, local copies, waits for them, and re-layouts: none -> 8.81 us
    pallas_call x1, Pallas kernels: 71.2 us -> 68 us  [local(): pl.pallas_call(layer_kernel, out_shape=(jax.ShapeDtypeStruct((1024, hid),...]
where the time goes in v4:
time: 80.6 us; the launch traced here: 80.2 us
  Pallas kernels  70.1 us (87%)
  local copies, waits for them, and re-layouts  8.81 us (11%)
  between operations  1.31 us (2%)
    pallas_call x1, Pallas kernels, local(): pl.pallas_call(layer_kernel, out_shape=(jax.ShapeDtypeStruct((1024, hid),...  68 us
    unnamed x22, local copies, waits for them, and re-layouts  8.81 us
    pallas_call x1, Pallas kernels, local(): pl.pallas_call(hand_on_kernel, out_shape=tuple((jax.ShapeDtypeStruct(r.sh...  2.08 us

profile of v4, /device:TPU:1, one launch (start us, length us, event | category | flops | bytes accessed | tf_op | source)
XLA Modules:
  0.0 80.2 jit_solution(15889210803935773848)
XLA Ops:
  1.3 0.0 copy-start
  1.3 1.2 %copy-done = s32[1024,256]{1,0:T(8,128)S(1)} copy-done((s32[1024,256]{1,0:T(8,128)S(1)}, s32[1024,256]{1,0:T(8,128)}, u32[]{:S(2)}) %copy-start) | copy-done | bytes 1048600
  2.5 0.0 copy-start.1
  2.5 1.0 %copy-done.1 = bf16[1024,256]{1,0:T(8,128)(2,1)S(1)} copy-done((bf16[1024,256]{1,0:T(8,128)(2,1)S(1)}, bf16[1024,256]{1,0:T(8,128)(2,1)}, u32[]{:S(2)}) %copy-start.1) | copy-done | bytes 524312
  3.5 0.0 copy-start.3
  3.5 0.9 %copy-done.3 = bf16[1024,128]{1,0:T(8,128)(2,1)S(1)} copy-done((bf16[1024,128]{1,0:T(8,128)(2,1)S(1)}, bf16[1024,128]{1,0:T(8,128)(2,1)}, u32[]{:S(2)}) %copy-start.3) | copy-done | bytes 262168
  4.5 0.0 copy-start.6
  4.5 0.8 %copy-done.6 = bf16[128,256]{1,0:T(8,128)(2,1)S(1)} copy-done((bf16[128,256]{1,0:T(8,128)(2,1)S(1)}, bf16[128,256]{1,0:T(8,128)(2,1)}, u32[]{:S(2)}) %copy-start.6) | copy-done | bytes 65560
  5.3 0.0 copy-start.7
  5.3 0.7 copy-done.7
  6.0 0.0 copy-start.8
  6.0 0.7 copy-done.8
  6.7 0.0 copy-start.9
  6.7 0.7 copy-done.9
  7.4 68.0 %layer.1 = (bf16[1024,256]{1,0:T(8,128)(2,1)S(1)}, bf16[8,128,128]{2,1,0:T(8,128)(2,1)S(1)}, f32[128,256]{1,0:T(8,128)S(1)}, f32[1,256]{1,0:T(1,128)S(1)}) custom-call(s32[1,1]{1,0:T(1,128)S(6)} %copy.13.count_ref, s32[1,256]{1,0:T(1,128)S(1)} %bitcast.8, s32[1,256]{1,0:T(1,128)S(1)} %bitcast.9, bf16[8,128,128]{2,1,0:T(8,128)(2,1)S(1)} %bitcast.7, ...), custom_call_target="tpu_custom_call" | custom-call | tf_op jit(solution)/shard_map/layer/pallas_call | solution.py:552
  75.4 0.0 copy-start.2
  75.4 0.8 copy-done.2
  76.2 0.0 copy-start.4
  76.2 0.7 copy-done.4
  76.9 0.0 copy-start.5
  76.9 0.7 copy-done.5
  77.5 0.0 copy-start.10
  77.5 0.6 copy-done.10
  78.1 2.1 %hand_on.1 = (bf16[1024,256]{1,0:T(8,128)(2,1)}, bf16[8,128,128]{2,1,0:T(8,128)(2,1)}, f32[128,256]{1,0:T(8,128)}, f32[1,256]{1,0:T(1,128)}) custom-call(bf16[1024,256]{1,0:T(8,128)(2,1)} %copy-done.2, bf16[8,128,128]{2,1,0:T(8,128)(2,1)} %copy-done.4, f32[128,256]{1,0:T(8,128)} %copy-done.5, f32[1,256]{1,0:T(1,128)} %copy-done.10), custom_call_target="tpu_custom_call" | custom-call | tf_op jit(solution)/shard_map/hand_on/pallas_call | solution.py:568
Async XLA Ops:
  1.3 1.2 %copy-start = (s32[1024,256]{1,0:T(8,128)S(1)}, s32[1024,256]{1,0:T(8,128)}, u32[]{:S(2)}) copy-start(s32[1024,256]{1,0:T(8,128)} %mask_hbm.1) | copy-start | bytes 3145732
  2.5 1.0 %copy-start.1 = (bf16[1024,256]{1,0:T(8,128)(2,1)S(1)}, bf16[1024,256]{1,0:T(8,128)(2,1)}, u32[]{:S(2)}) copy-start(bf16[1024,256]{1,0:T(8,128)(2,1)} %cot_hbm.1) | copy-start | bytes 1572868
  3.5 0.9 %copy-start.3 = (bf16[1024,128]{1,0:T(8,128)(2,1)S(1)}, bf16[1024,128]{1,0:T(8,128)(2,1)}, u32[]{:S(2)}) copy-start(bf16[1024,128]{1,0:T(8,128)(2,1)} %param.9) | copy-start | bytes 786436
  4.5 0.8 %copy-start.6 = (bf16[128,256]{1,0:T(8,128)(2,1)S(1)}, bf16[128,256]{1,0:T(8,128)(2,1)}, u32[]{:S(2)}) copy-start(bf16[128,256]{1,0:T(8,128)(2,1)} %weight_ref.1) | copy-start | bytes 196612
  5.3 0.7 copy-start.7
  6.0 0.7 copy-start.8
  6.7 0.7 copy-start.9
  75.4 0.8 %copy-start.2 = (bf16[1024,256]{1,0:T(8,128)(2,1)}, bf16[1024,256]{1,0:T(8,128)(2,1)S(1)}, u32[]{:S(2)}) copy-start(bf16[1024,256]{1,0:T(8,128)(2,1)S(1)} %get-tuple-element.12.refs_0_) | copy-start | bytes 1572868
  76.2 0.7 copy-start.4
  76.9 0.7 copy-start.5
  77.5 0.6 copy-start.10

commit v5 on v4

--- a/solution.py
+++ b/solution.py
@@ -85,8 +85,9 @@
 
 
 def layer_kernel(
-    count_ref, rows_ref, cols_ref, feat_ref, weight_ref, bias_ref, cot_hbm, mask_hbm, adj_ref,
-    out_ref, gf_ref, gw_ref, gb_ref,
+    count_ref, rows_hbm, cols_hbm, feat_hbm, weight_hbm, bias_hbm, cot_hbm, mask_hbm, adj_ref,
+    out_hbm, gf_hbm, gw_hbm, gb_hbm,
+    rows_ref, cols_ref, weight_ref, bias_ref, out_ref, gf_ref, gw_ref, gb_ref,
     idx_vmem, flt_vmem, idx_ref, flt_ref, cot_ref, mask_ref, adj, run, feats, proj, gpre, rsend, crecv, rown,
     zs1, zr1, zs2, zr2, zxs, zxr, ys1, yr1, ys2, yr2, yxs, yxr,
     agg, gsum, ar_col, ar_row, gall, bias_own, bias_col, bias_row,
@@ -119,17 +120,23 @@
                 to_xh, to_y = (xh + flip) % 2, (y + step) % 4
                 row_mates.append((dev(xh=to_xh, y=to_y), to_xh * 4 + to_y))
     partners = [mate for mate, _ in row_mates + col_mates]
+    feat_copy = pltpu.make_async_copy(feat_hbm, feats.at[pl.ds(row * SHARD, SHARD)], in_sems.at[5])
+    weight_copy = pltpu.make_async_copy(weight_hbm, weight_ref, in_sems.at[6])
     cot_copy = pltpu.make_async_copy(cot_hbm, cot_ref, in_sems.at[0])
     mask_copy = pltpu.make_async_copy(mask_hbm, mask_ref, in_sems.at[1])
+    rows_copy = pltpu.make_async_copy(rows_hbm, rows_ref, in_sems.at[8])
+    cols_copy = pltpu.make_async_copy(cols_hbm, cols_ref, in_sems.at[9])
+    bias_copy = pltpu.make_async_copy(bias_hbm, bias_ref, in_sems.at[7])
     adj_copy = pltpu.make_async_copy(adj_ref, adj, in_sems.at[2])
-    for copy in (cot_copy, mask_copy, adj_copy):
-        copy.start()
 
     barrier = pltpu.get_barrier_semaphore()
     for partner in partners:
         pl.semaphore_signal(barrier, inc=1, device_id=partner, device_id_type=MESH)
+    for copy in (cot_copy, mask_copy, weight_copy, feat_copy, rows_copy, cols_copy, bias_copy, adj_copy):
+        copy.start()
 
     gb_ref[...] = jnp.zeros_like(gb_ref)
+    weight_copy.wait()
     cot_copy.wait()
     mask_copy.wait()
 
@@ -216,7 +223,8 @@
             lines.wait(table[d], place, self.ring(step))
             return place
 
-    rows_g = Gather(feats, lambda h: feat_ref.at[pl.ds(h * HALF, HALF)],
+    feat_copy.wait()
+    rows_g = Gather(feats, lambda h: part(feats, row, h),
                     lambda pair, pos: pair * 4 + pos, y, xh, at_y, pair_x)
     rows_g.begin()
 
@@ -234,10 +242,10 @@
         there = part(proj, (pair * 4 + (z + step) % 4) * 2 + 1 - core, h)
         across.append((line, there))
 
-    feats[pl.ds(row * SHARD, SHARD)] = feat_ref[...]
-
     cross(0, 0, 0)
     cross(0, 0, 1)
+    for copy in (rows_copy, cols_copy, bias_copy):
+        copy.wait()
     plan(count_ref, rows_ref, cols_ref, idx_vmem, flt_vmem)
     idx_copy = pltpu.make_async_copy(idx_vmem, idx_ref, in_sems.at[3])
     flt_copy = pltpu.make_async_copy(flt_vmem, flt_ref, in_sems.at[4])
@@ -352,10 +360,11 @@
             self.term, self.ring, self.mate, self.far_by_mate = term, ring, mate, far_by_mate
             self.l1 = [[lines.line() for _ in range(2)] for _ in range(2)]
             self.l2 = [[[lines.line() for _ in range(2)] for _ in range(2)] for _ in range(2)]
+            self.l2b = [lines.line() for _ in range(2)]
             self.lx = [lines.line() for _ in range(2)]
 
-        def far(self, pair_step):
-            for d in range(2):
+        def far(self, pair_step, ways=(0, 1)):
+            for d in ways:
                 if self.far_by_mate and pair_step == 0:
                     lines.wait(self.l1[1][d], self.r1.at[pl.ds(SHARD + d * HALF, HALF)], self.mate)
 
@@ -372,29 +381,36 @@
                 lines.send(self.l1[pair_step][d], self.s1.at[place], self.r1.at[place],
                            self.mate if self.far_by_mate and pair_step else self.ring(1 - 2 * d))
 
-        def near(self, pair_step, d, late):
+        def near(self, pair_step, d, late, cut=None):
             h = d if late else 1 - d
-            base = (pair_step * 2 + d) * SHARD + h * HALF
+            first = h * HALF + (cut or 0) * (HALF // 2)
+            count = HALF if cut is None else HALF // 2
+            base = (pair_step * 2 + d) * SHARD + first
+            line = self.l2b[d] if cut else self.l2[pair_step][d][h]
             passing = late and not (self.far_by_mate and pair_step)
             if passing:
                 place = pl.ds(pair_step * SHARD + d * HALF, HALF)
                 lines.wait(self.l1[pair_step][d], self.r1.at[place], self.ring(2 * d - 1))
 
             def fill(b, _):
-                value = self.term(pair_step, 1 - 2 * d, h * HALF + b)
+                value = self.term(pair_step, 1 - 2 * d, first + b)
                 if passing:
                     value = value + self.r1[pair_step * SHARD + d * HALF + b].astype(F32)
                 self.s2[base + b] = value.astype(BF16)
                 return 0
 
-            lax.fori_loop(0, HALF, fill, 0, unroll=HALF)
-            place = pl.ds(base, HALF)
-            lines.send(self.l2[pair_step][d][h], self.s2.at[place], self.r2.at[place], self.ring(1 - 2 * d))
+            lax.fori_loop(0, count, fill, 0, unroll=count)
+            place = pl.ds(base, count)
+            lines.send(line, self.s2.at[place], self.r2.at[place], self.ring(1 - 2 * d))
 
         def wait_near(self, pair_step, h):
             for d in range(2):
-                place = pl.ds((pair_step * 2 + d) * SHARD + h * HALF, HALF)
-                lines.wait(self.l2[pair_step][d][h], self.r2.at[place], self.ring(2 * d - 1))
+                base = (pair_step * 2 + d) * SHARD + h * HALF
+                if pair_step == 0 and h == 1 - d:
+                    for cut, line in enumerate((self.l2[0][d][h], self.l2b[d])):
+                        lines.wait(line, self.r2.at[pl.ds(base + cut * (HALF // 2), HALF // 2)], self.ring(2 * d - 1))
+                else:
+                    lines.wait(self.l2[pair_step][d][h], self.r2.at[pl.ds(base, HALF)], self.ring(2 * d - 1))
 
         def total(self, pair_step, b):
             base = pair_step * 2 * SHARD + b
@@ -435,7 +451,7 @@
         rows_s.near(1, d, True)
     for d in range(2):
         add_core(0, 1 - 2 * d)
-        rows_s.near(0, d, False)
+        rows_s.near(0, d, False, 0)
     add_core(0, 2)
     for pair_step in (1, 0):
         add_core(pair_step, 0)
@@ -464,14 +480,17 @@
     cols_s.far(1)
     for d in range(2):
         cols_s.near(1, d, False)
-    rows_s.far(0)
+    for d in range(2):
+        rows_s.far(0, (d,))
+        rows_s.near(0, d, False, 1)
     for h in range(2):
         rows_s.swap(h)
     for d in range(2):
         cols_s.near(1, d, True)
     cols_s.far(0)
     for d in range(2):
-        cols_s.near(0, d, False)
+        for cut in range(2):
+            cols_s.near(0, d, False, cut)
     for d in range(2):
         rows_s.near(0, d, True)
 
@@ -503,6 +522,8 @@
     used = spread(col_mates, lambda theirs: gsum.at[theirs], ar_col, col)
     ar_col[col] = gsum[col]
     lax.fori_loop(0, SHARD, layer, 0, unroll=SHARD)
+    out_copy = pltpu.make_async_copy(out_ref, out_hbm, in_sems.at[10])
+    out_copy.start()
     for h in range(2):
         cols_s.swap(h)
     for d in range(2):
@@ -519,13 +540,21 @@
 
     for h in range(2):
         cols_s.finish(h, store)
+    gf_copy = pltpu.make_async_copy(gf_ref, gf_hbm, in_sems.at[11])
+    gf_copy.start()
 
     collect(row_mates, bias_lines, bias_row)
     gb_ref[...] = added(bias_row)
     collect(col_mates, used, gall)
     for n in range(pieces):
         gw_ref[pl.ds(n * depth, depth), :] = gall[n]
+    gw_copy = pltpu.make_async_copy(gw_ref, gw_hbm, in_sems.at[12])
+    gb_copy = pltpu.make_async_copy(gb_ref, gb_hbm, in_sems.at[13])
+    gw_copy.start()
+    gb_copy.start()
     lines.drain()
+    for copy in (out_copy, gf_copy, gw_copy, gb_copy):
+        copy.wait()
     assert lines.used <= N_LINES
 
 
@@ -539,6 +568,8 @@
 
     plan_shape = (8, slots)
     scratch = [
+        pltpu.VMEM((1, slots), jnp.int32), pltpu.VMEM((1, slots), jnp.int32), pltpu.VMEM(weight.shape, BF16), pltpu.VMEM((1, hid), F32),
+        pltpu.VMEM((1024, hid), BF16), pltpu.VMEM((SHARD, BLK, BLK), BF16), pltpu.VMEM(weight.shape, F32), pltpu.VMEM((1, hid), F32),
         pltpu.VMEM(plan_shape, jnp.int32), pltpu.VMEM(plan_shape, F32), pltpu.SMEM(plan_shape, jnp.int32), pltpu.SMEM(plan_shape, F32),
         pltpu.VMEM((1024, hid), BF16), pltpu.VMEM((1024, hid), jnp.int32),
         blocks(slots), blocks(slots, F32), blocks(64), blocks(128), pltpu.VMEM((1024, hid), BF16),
@@ -548,7 +579,7 @@
     piece = (8, hid)
     scratch += [blocks(8)] + [pltpu.VMEM((n,) + piece, F32) for n in (16, 16, 8, 16)]
     scratch += [pltpu.VMEM((n, 1, hid), F32) for n in (1, 16, 8)]
-    scratch += [pltpu.SemaphoreType.DMA((N_LINES,)), pltpu.SemaphoreType.DMA((N_LINES,)), pltpu.SemaphoreType.DMA((5,))]
+    scratch += [pltpu.SemaphoreType.DMA((N_LINES,)), pltpu.SemaphoreType.DMA((N_LINES,)), pltpu.SemaphoreType.DMA((14,))]
     out, gf, gw, gb = pl.pallas_call(
         layer_kernel,
         out_shape=(
@@ -557,10 +588,10 @@
             jax.ShapeDtypeStruct(weight.shape, F32),
             jax.ShapeDtypeStruct((1, hid), F32),
         ),
-        in_specs=[smem, vmem, vmem, vmem, vmem, vmem, hbm, hbm, hbm],
-        out_specs=(vmem, vmem, vmem, vmem),
+        in_specs=[smem] + [hbm] * 8,
+        out_specs=(hbm,) * 4,
         scratch_shapes=scratch,
-        compiler_params=pltpu.CompilerParams(collective_id=0, has_side_effects=True, vmem_limit_bytes=51 * 2**20),
+        compiler_params=pltpu.CompilerParams(collective_id=0, has_side_effects=True, vmem_limit_bytes=60 * 2**20),
         name="layer",
     )(block_count, block_rows[0], block_cols[0], features.reshape(SHARD, BLK, BLK), weight, bias.reshape(1, hid), cotangent, relu_mask,
       adjacency.reshape(slots, BLK, BLK))

time: 80.6 us -> 71 us (0.88)
  local copies, waits for them, and re-layouts: 8.81 us -> 0 us
    unnamed x22 -> x0, local copies, waits for them, and re-layouts: 8.81 us -> none
where the time goes in v5:
time: 71 us; the launch traced here: 70.9 us
  Pallas kernels  69.6 us (98%)
  between operations  1.29 us (2%)
    pallas_call x1, Pallas kernels, local(): pl.pallas_call(layer_kernel, out_shape=(jax.ShapeDtypeStruct((1024, hid),...  67.5 us
    pallas_call x1, Pallas kernels, local(): pl.pallas_call(hand_on_kernel, out_shape=tuple((jax.ShapeDtypeStruct(r.sh...  2.08 us

profile of v5, /device:TPU:1, one launch (start us, length us, event | category | flops | bytes accessed | tf_op | source)
XLA Modules:
  0.0 70.9 jit_solution(9535684751213681097)
XLA Ops:
  1.3 67.5 %layer.1 = (bf16[1024,256]{1,0:T(8,128)(2,1)}, bf16[8,128,128]{2,1,0:T(8,128)(2,1)}, f32[128,256]{1,0:T(8,128)}, f32[1,256]{1,0:T(1,128)}) custom-call(s32[1,1]{1,0:T(1,128)S(6)} %copy.13.count_ref, s32[1,256]{1,0:T(1,128)} %bitcast.9, s32[1,256]{1,0:T(1,128)} %bitcast.10, bf16[8,128,128]{2,1,0:T(8,128)(2,1)} %bitcast.8, bf16[128,256]{1,0:T(8,128)(2,1)} %weight_hbm.1, ...), custom_call_target="tpu_custom_call" | custom-call | tf_op jit(solution)/shard_map/layer/pallas_call | solution.py:583
  68.8 2.1 %hand_on.1 = (bf16[1024,256]{1,0:T(8,128)(2,1)}, bf16[8,128,128]{2,1,0:T(8,128)(2,1)}, f32[128,256]{1,0:T(8,128)}, f32[1,256]{1,0:T(1,128)}) custom-call(bf16[1024,256]{1,0:T(8,128)(2,1)} %get-tuple-element.12.refs_0_, bf16[8,128,128]{2,1,0:T(8,128)(2,1)} %get-tuple-element.13.refs_1_, f32[128,256]{1,0:T(8,128)} %get-tuple-element.14.refs_2_, ...), custom_call_target="tpu_custom_call" | custom-call | tf_op jit(solution)/shard_map/hand_on/pallas_call | solution.py:599

commit v6 on v5

--- a/solution.py
+++ b/solution.py
@@ -321,7 +321,7 @@
         run[p] = total
         return total
 
-    lax.fori_loop(0, slots, forward, jnp.zeros((BLK, BLK), F32), unroll=64)
+    lax.fori_loop(0, slots, forward, jnp.zeros((BLK, BLK), F32), unroll=128)
 
     def row_block(b):
         return run[idx_ref[2, b]] * flt_ref[1, b]
@@ -494,10 +494,6 @@
     for d in range(2):
         rows_s.near(0, d, True)
 
-    collect(col_mates, bias_lines, bias_col)
-    bias_row[row] = added(bias_col)
-    bias_lines = spread(row_mates, lambda theirs: bias_row.at[row], bias_row, row)
-
     def aggregate(b, value):
         agg[b] = value.astype(BF16)
 
@@ -521,6 +517,9 @@
         gsum[n] = gw_ref[pl.ds(n * depth, depth), :]
     used = spread(col_mates, lambda theirs: gsum.at[theirs], ar_col, col)
     ar_col[col] = gsum[col]
+    collect(col_mates, bias_lines, bias_col)
+    bias_row[row] = added(bias_col)
+    bias_lines = spread(row_mates, lambda theirs: bias_row.at[row], bias_row, row)
     lax.fori_loop(0, SHARD, layer, 0, unroll=SHARD)
     out_copy = pltpu.make_async_copy(out_ref, out_hbm, in_sems.at[10])
     out_copy.start()

time: 71 us -> 70.7 us (level)
  no operation moved by 1% of the time
where the time goes in v6:
time: 70.7 us; the launch traced here: 70.6 us
  Pallas kernels  69.3 us (98%)
  between operations  1.29 us (2%)
    pallas_call x1, Pallas kernels, local(): pl.pallas_call(layer_kernel, out_shape=(jax.ShapeDtypeStruct((1024, hid),...  67.2 us
    pallas_call x1, Pallas kernels, local(): pl.pallas_call(hand_on_kernel, out_shape=tuple((jax.ShapeDtypeStruct(r.sh...  2.08 us

profile of v6, /device:TPU:1, one launch (start us, length us, event | category | flops | bytes accessed | tf_op | source)
XLA Modules:
  0.0 70.6 jit_solution(9819143214002080780)
XLA Ops:
  1.3 67.2 %layer.1 = (bf16[1024,256]{1,0:T(8,128)(2,1)}, bf16[8,128,128]{2,1,0:T(8,128)(2,1)}, f32[128,256]{1,0:T(8,128)}, f32[1,256]{1,0:T(1,128)}) custom-call(s32[1,1]{1,0:T(1,128)S(6)} %copy.13.count_ref, s32[1,256]{1,0:T(1,128)} %bitcast.9, s32[1,256]{1,0:T(1,128)} %bitcast.10, bf16[8,128,128]{2,1,0:T(8,128)(2,1)} %bitcast.8, bf16[128,256]{1,0:T(8,128)(2,1)} %weight_hbm.1, ...), custom_call_target="tpu_custom_call" | custom-call | tf_op jit(solution)/shard_map/layer/pallas_call | solution.py:582
  68.5 2.1 %hand_on.1 = (bf16[1024,256]{1,0:T(8,128)(2,1)}, bf16[8,128,128]{2,1,0:T(8,128)(2,1)}, f32[128,256]{1,0:T(8,128)}, f32[1,256]{1,0:T(1,128)}) custom-call(bf16[1024,256]{1,0:T(8,128)(2,1)} %get-tuple-element.12.refs_0_, bf16[8,128,128]{2,1,0:T(8,128)(2,1)} %get-tuple-element.13.refs_1_, f32[128,256]{1,0:T(8,128)} %get-tuple-element.14.refs_2_, ...), custom_call_target="tpu_custom_call" | custom-call | tf_op jit(solution)/shard_map/hand_on/pallas_call | solution.py:598
